TPU v7x, 32 devices: a whole 2x2x4 slice. The times are simulated.
32 devices in a mesh: tm: 4 (over z), pairs: 8 (over y, x, core).
Axes of the slice: x: 2, y: 2, z: 4, core: 2. Of those that a mesh axis runs over, the one named last changes fastest.
Arguments:
- record: bfloat16 [32, 3, 4, 4096], P('pairs', None, 'tm')
- requested: int32 [8, 8, 2], replicated, may hold values from 0 to 3, as said below
- partners: int32 [8, 12, 48], P('pairs'), may hold values from 0 to 15
- codes: int32 [8, 12, 48], P('pairs'), may hold values from 0 to 2
- counts: int32 [8, 12], P('pairs'), may hold values from 1 to 48, as said below
Outputs:
- stacks: float32 [8, 576, 1024], P('pairs', 'tm')
Inputs may be any that keep to these rules, and one draw needn't show every extreme that they name: requested[e, d] holds 2 different local station indices of device d, meaning stations d * 4 + requested[e, d, i]. `partners`: slot k stands for the station requested[e, k // 2, k % 2]. Slots at and after counts[e, j] are unused; on some device every owned trace has 48 live slots.
All inputs are finite; a program needn't handle non-finite values.
Results may differ from a plain program's by a relative error of at most 0.0037.
Values may be sent and summed in bfloat16 or wider, within the bound.
A program may use at most 64 MiB of HBM per device.

v0:
```python
import math

import jax
import jax.numpy as jnp
from jax import lax
from jax.sharding import PartitionSpec as P

LAGS = 1024


def normalize(traces):
    values = traces.astype(jnp.float32)
    values = values - jnp.mean(values, axis=-1, keepdims=True)
    power_mean = jnp.mean(values * values, axis=-1, keepdims=True)
    return (values * lax.rsqrt(power_mean + 1e-06)).astype(jnp.bfloat16)


def correlate(own_trace, partner_rows, lag_count, block_len):
    window_len = own_trace.shape[0]
    half_lag = lag_count // 2
    padded = jnp.pad(own_trace, (half_lag, half_lag + block_len))
    length = padded.shape[0]
    spread = jnp.broadcast_to(padded, (block_len, length)).reshape(-1)
    spread = jnp.pad(spread, (0, block_len))
    skewed = spread.reshape(block_len, length + 1)[:, : window_len + lag_count]
    hankel = skewed.reshape(block_len, (window_len + lag_count) // block_len, block_len)
    blocks_in = window_len // block_len
    pieces = partner_rows.reshape(partner_rows.shape[0], blocks_in, block_len)
    outputs = []
    for offset in range(lag_count // block_len):
        window_view = hankel[:, offset : offset + blocks_in, :]
        outputs.append(
            jnp.einsum("pmi,imr->pr", pieces, window_view, preferred_element_type=jnp.float32)
        )
    return jnp.concatenate(outputs, axis=1)


def shards(record, requested, partners, codes, counts):
    whitened = normalize(record)
    local_stations, comp_count, window_count, window_len = whitened.shape
    owners = lax.axis_size("pairs")
    capacity = requested.shape[2]
    per_trace = partners.shape[2]
    trace_count = local_stations * comp_count
    block_len = math.gcd(math.gcd(128, window_len), LAGS)
    own_index = lax.axis_index("pairs")
    slot_ids = partners[0]
    comp_ids = codes[0]
    everyone = lax.all_gather(whitened, "pairs", axis=0, tiled=True)
    trace_pool = everyone.reshape(owners * local_stations * comp_count, window_count, window_len)
    asked_table = lax.dynamic_index_in_dim(requested, own_index, axis=0, keepdims=False)
    station_of = (
        asked_table + jnp.arange(owners, dtype=jnp.int32)[:, None] * local_stations
    ).reshape(-1)
    matches = slot_ids[:, :, None] == jnp.arange(owners * capacity, dtype=jnp.int32)[None, None, :]
    stations = jnp.sum(jnp.where(matches, station_of[None, None, :], 0), axis=-1)
    row_ids = stations * comp_count + comp_ids
    picked = jnp.take(trace_pool, row_ids.reshape(-1), axis=0)
    live_rows = jnp.arange(per_trace, dtype=jnp.int32)[None, :] < counts[0][:, None]
    picked = jnp.where(live_rows.reshape(-1)[:, None, None], picked, jnp.zeros((), jnp.bfloat16))
    picked = picked.reshape(trace_count, per_trace, window_count, window_len)
    picked = jnp.moveaxis(picked, 2, 1).reshape(trace_count * window_count, per_trace, window_len)
    own_rows = whitened.reshape(trace_count * window_count, window_len)

    def one_trace(operands):
        own_row, partner_rows = operands
        return correlate(own_row, partner_rows, LAGS, block_len)

    lagged = lax.map(one_trace, (own_rows, picked))
    lagged = lagged.reshape(trace_count, window_count, per_trace, LAGS)
    total_windows = window_count * lax.axis_size("tm")
    window_term = jnp.sum(lagged, axis=1) * (1.0 / math.sqrt(window_len * total_windows))
    window_term = window_term.reshape(1, trace_count * per_trace, LAGS)
    return lax.psum_scatter(window_term, "tm", scatter_dimension=1, tiled=True)


def solution(mesh):
    return jax.shard_map(
        shards,
        mesh=mesh,
        in_specs=(
            P("pairs", None, "tm", None),
            P(),
            P("pairs", None, None),
            P("pairs", None, None),
            P("pairs", None),
        ),
        out_specs=P("pairs", "tm", None),
        check_vma=False,
    )
```

profile of v0, /device:TPU:0, one launch (start us, length us, event | category | flops | bytes accessed | tf_op | source)
XLA Modules:
  0.0 218.2 jit_solution(2879049199075822810)
XLA Ops:
  9.8 12.4 %all_gather.3 = bf16[32,3,1,4096]{3,1,2,0:T(4,128)(2,1)S(1)} all-gather(bf16[4,3,1,4096]{3,1,2,0:T(4,128)(2,1)S(1)} %fusion.27), channel_id=1, replica_groups=mesh['tm'=4,'pairs'=8] {'pairs'}, dimensions={0}, use_global_device_ids=true | all-gather | bytes 884736 | tf_op jit(solution)/shard_map/all_gather | solution.py:49
  25.2 5.3 %gather_fusion = bf16[576,4096]{1,0:T(8,128)(2,1)} fusion(bf16[96,4096]{1,0:T(8,128)(2,1)S(1)} %reshape.160, s32[1024]{0:T(1024)S(1)} %pad_clamp_fusion), kind=kCustom, calls=%fused_computation | custom fusion | bytes 9439488 | tf_op jit(solution)/shard_map/jit(_take)/gather | solution.py:58
  30.5 5.1 %select_select_fusion = bf16[12,48,4096]{2,1,0:T(8,128)(2,1)} fusion(bf16[12,48,4096]{2,1,0:T(8,128)(2,1)} %bitcast.87, pred[12,48]{1,0:T(8,128)(4,1)S(1)} %get-tuple-element.68, pred[12,48]{1,0:T(8,128)(4,1)S(1)} %get-tuple-element.67), kind=kLoop, calls=%fused_computation.36 | loop fusion | flops 4718592 | bytes 9438336 | tf_op jit(solution)/shard_map/jit(_where)/select_n | solution.py:60
  35.6 123.7 %while.12 = (s32[]{:T(128)}, f32[12,48,1024]{2,1,0:T(8,128)}, bf16[12,48,4096]{2,1,0:T(8,128)(2,1)}, bf16[12,4096]{1,0:T(8,128)(2,1)S(1)}, s32[]{:T(128)}, /*index=5*/bf16[]{:T(256)}) while((s32[]{:T(128)}, f32[12,48,1024]{2,1,0:T(8,128)}, bf16[12,48,4096]{2,1,0:T(8,128)(2,1)}, bf16[12,4096]{1,0:T(8,128)(2,1)S(1)}, s32[]{:T(128)}, ...), condition=%wide.region_4.5_spmd, body=%wide.region_3.4_spmd.sunk | while | flops 402653184 | bytes 28391248 | solution.py:69
  35.8 1.5 reshape.185
  37.4 2.0 reshape.186
  46.1 1.5 reshape.185
  47.8 2.0 reshape.186
  56.4 1.5 reshape.185
  58.0 2.0 reshape.186
  66.7 1.5 reshape.185
  68.3 2.0 reshape.186
  77.0 1.5 reshape.185
  78.7 2.0 reshape.186
  89.0 2.0 reshape.186
  99.3 2.0 reshape.186
  109.6 2.0 reshape.186
  119.9 2.0 reshape.186
  130.2 2.0 reshape.186
  138.9 1.5 reshape.185
  140.5 2.0 reshape.186
  150.8 2.0 reshape.186
  159.3 3.5 %broadcast_multiply_fusion = f32[12,48,1024]{2,1,0:T(8,128)} fusion(f32[12,48,1024]{2,1,0:T(8,128)} %get-tuple-element.58), kind=kLoop, calls=%fused_computation.37 | loop fusion | flops 589824 | bytes 4718592 | tf_op jit(solution)/shard_map/mul | solution.py:72
  162.8 48.5 %reduce-scatter.2.cloned.1.call-done = f32[1,144,1024]{2,1,0:T(8,128)} async-done(((f32[1,576,1024]{2,1,0:T(8,128)}), f32[1,144,1024]{2,1,0:T(8,128)}) %reduce-scatter.2.cloned.1.call-update) | async-done | bytes 589840 | tf_op jit(solution)/shard_map/reduce_scatter | solution.py:74
  (242 shorter events, 95.4 us)
Async XLA Ops:
  6.5 15.8 %copy-start = (s32[8,8,2]{1,2,0:T(2,128)S(1)}, s32[8,8,2]{1,2,0:T(2,128)}, u32[]{:S(2)}) copy-start(s32[8,8,2]{1,2,0:T(2,128)} %param.8) | copy-start | bytes 1540
  6.5 18.6 %copy-start.1 = (s32[1,12,48]{2,0,1:T(1,128)S(1)}, s32[1,12,48]{2,0,1:T(1,128)}, u32[]{:S(2)}) copy-start(s32[1,12,48]{2,0,1:T(1,128)} %param.10) | copy-start | bytes 6916
  6.5 18.6 %copy-start.2 = (s32[1,12]{1,0:T(1,128)S(1)}, s32[1,12]{1,0:T(1,128)}, u32[]{:S(2)}) copy-start(s32[1,12]{1,0:T(1,128)} %param.11) | copy-start | bytes 148
  6.5 204.8 %reduce-scatter.2.cloned.1.call-start = ((), (), s32[]{:S(2)}) async-start(), calls=%async_computation.1 | async-start | bytes 2949120 | tf_op jit(solution)/shard_map/reduce_scatter | solution.py:74
Sparse Core Ops, SparseCore 0:
  162.9 48.3 reduce-scatter.1
where the time goes:
time: 219 us; the launch traced here: 218 us
  local copies, waits for them, and re-layouts  85.1 us (39%)
  waiting for transfers between devices  48.5 us (22%)
  matrix products  44.5 us (20%)
  between operations  13.5 us (6%)
  other arithmetic  12.8 us (6%)
  blocking collectives  12.4 us (6%)
    reduce_scatter x1, waiting for transfers between devices, shards(): return lax.psum_scatter(window_term, 'tm', scatter_dimension=1, tiled=True)  48.5 us
    dot_general x96, matrix products, correlate(): jnp.einsum('pmi,imr->pr', pieces, window_view, preferred_element_type=jnp...  44.5 us
    reshape x12, local copies, waits for them, and re-layouts, correlate(): skewed = spread.reshape(block_len, length + 1)[:, :window_len + lag_count]  23.9 us
    reshape x12, local copies, waits for them, and re-layouts, correlate(): spread = jnp.broadcast_to(padded, (block_len, length)).reshape(-1)  18.6 us
    while x24, local copies, waits for them, and re-layouts  13.1 us
    all_gather x1, blocking collectives, shards(): everyone = lax.all_gather(whitened, 'pairs', axis=0, tiled=True)  12.4 us
    slice x24, local copies, waits for them, and re-layouts, correlate(): skewed = spread.reshape(block_len, length + 1)[:, :window_len + lag_count]  10.8 us
    dynamic_update_slice x12, local copies, waits for them, and re-layouts, shards(): lagged = lax.map(one_trace, (own_rows, picked))  8.4 us
  transfers between devices with their start and end apart: 1, of which 1 were waited for; matrix products, arithmetic and copies ran while one was open for 0% of the time, Pallas kernels for 0%

commit v1 on v0

--- a/solution.py
+++ b/solution.py
@@ -1,8 +1,11 @@
+import functools
 import math
 
 import jax
 import jax.numpy as jnp
 from jax import lax
+from jax.experimental import pallas as pl
+from jax.experimental.pallas import tpu as pltpu
 from jax.sharding import PartitionSpec as P
 
 LAGS = 1024
@@ -74,9 +77,319 @@
     return lax.psum_scatter(window_term, "tm", scatter_dimension=1, tiled=True)
 
 
+MESH = pl.DeviceIdType.MESH
+HALF = 128
+BLOCK = 2 * HALF
+FROM_X, FROM_Y, DIAG_A, DIAG_B, CORE_OWN, CORE_X, CORE_Y, CORE_D = range(8)
+
+
+def xor_step(t, k):
+    if k == 1:
+        return t + 1 - 2 * lax.rem(t, 2)
+    if k == 2:
+        return lax.rem(t + 2, 4)
+    return 3 - t
+
+
+def exchange_kernel(
+    dims, asked_ref, record_ref, cc_ref, *scratch
+):
+    traces, blocks_in, owners, capacity, comps, own_count, lag_blocks = dims
+    blks = scratch[:4]
+    (rows32, pool32, own32, lhs, hankel, acc, send, recv, zsend, zrecv) = scratch[4:]
+    pool = owners * capacity * comps
+    first_s, last_s = 1, blocks_in + lag_blocks - 3
+    t = lax.axis_index("tm")
+    e = lax.axis_index("pairs")
+    core, x, y = lax.rem(e, 2), lax.rem(e // 2, 2), e // 4
+    ex, ey, ec = e + 2 - 4 * x, e + 4 - 8 * y, e + 1 - 2 * core
+    ed = ex + 4 - 8 * y
+    cx, cy, cd = ex + 1 - 2 * core, ey + 1 - 2 * core, ed + 1 - 2 * core
+
+    barrier = pltpu.get_barrier_semaphore()
+    for peer in ((t, ex), (t, ey), (t, ec)) + tuple((xor_step(t, k), e) for k in (1, 2, 3)):
+        pl.semaphore_signal(barrier, inc=1, device_id=peer, device_id_type=MESH)
+
+    row_index = lax.broadcasted_iota(jnp.int32, (HALF, HALF), 0)
+    lane_index = lax.broadcasted_iota(jnp.int32, (HALF, HALF), 1)
+    mirror = jnp.where(row_index + lane_index == HALF - 1, 1.0, 0.0).astype(jnp.bfloat16)
+
+    def flip_halves(tile):
+        return jnp.dot(tile, mirror, preferred_element_type=jnp.float32)
+
+    values = record_ref[...].astype(jnp.float32)
+    values = values - jnp.mean(values, axis=-1, keepdims=True)
+    power_mean = jnp.mean(values * values, axis=-1, keepdims=True)
+    values = values * lax.rsqrt(power_mean + 1e-06)
+    for m in range(blocks_in):
+        for h in (0, 1):
+            lane = m * BLOCK + h * HALF
+            rows32[h, pl.ds(m, traces, stride=blocks_in), :] = values[:, lane : lane + HALF]
+    for h in (0, 1):
+        blks[0][e, :, :, h * HALF : (h + 1) * HALF] = (
+            flip_halves(rows32[h].astype(jnp.bfloat16))
+            .astype(jnp.bfloat16)
+            .reshape(traces, blocks_in, HALF)
+        )
+    pl.semaphore_wait(barrier, 6)
+
+    def plane_copy(k, kind, origin, target):
+        blk = blks[k]
+        if kind == DIAG_A:
+            ref = blk.at[origin, pl.ds(0, traces // 2)]
+        elif kind == DIAG_B:
+            ref = blk.at[origin, pl.ds(traces // 2, traces // 2)]
+        else:
+            ref = blk.at[origin]
+        return pltpu.make_async_remote_copy(
+            src_ref=ref, dst_ref=ref,
+            send_sem=send.at[k, kind], recv_sem=recv.at[k, kind],
+            device_id=(t, target), device_id_type=MESH,
+        )
+
+    def z_copy(k):
+        return pltpu.make_async_remote_copy(
+            src_ref=blks[0].at[e], dst_ref=blks[k].at[e],
+            send_sem=zsend.at[k - 1], recv_sem=zrecv.at[k - 1],
+            device_id=(xor_step(t, k), e), device_id_type=MESH,
+        )
+
+    def send_own(k):
+        plane_copy(k, FROM_X, e, ex).start()
+        plane_copy(k, FROM_Y, e, ey).start()
+        plane_copy(k, CORE_OWN, e, ec).start()
+
+    def forward_xy(k):
+        plane_copy(k, FROM_X, ex, ex).wait_recv()
+        plane_copy(k, DIAG_A, ex, ey).start()
+        plane_copy(k, CORE_X, ex, ec).start()
+        plane_copy(k, FROM_Y, ey, ey).wait_recv()
+        plane_copy(k, DIAG_B, ey, ex).start()
+        plane_copy(k, CORE_Y, ey, ec).start()
+
+    def forward_diag(k):
+        plane_copy(k, DIAG_A, ed, ey).wait_recv()
+        plane_copy(k, DIAG_B, ed, ex).wait_recv()
+        plane_copy(k, CORE_D, ed, ec).start()
+
+    def wait_core(k):
+        plane_copy(k, CORE_OWN, ec, ec).wait_recv()
+        plane_copy(k, CORE_X, cx, ec).wait_recv()
+        plane_copy(k, CORE_Y, cy, ec).wait_recv()
+        plane_copy(k, CORE_D, cd, ec).wait_recv()
+
+    below = lane_index <= row_index
+    zeros = jnp.zeros((HALF, HALF), jnp.float32)
+
+    def put(j, s, row_half, lane_half, tile):
+        if first_s <= s <= last_s:
+            row = (s - first_s) * BLOCK + row_half * HALF
+            hankel[j, row : row + HALF, lane_half * HALF : (lane_half + 1) * HALF] = tile
+
+    def build(k):
+        def one(j, carry):
+            for h in (0, 1):
+                lanes = slice(h * HALF, (h + 1) * HALF)
+                own32[:, lanes] = flip_halves(blks[k][e, own_count * t + j, :, lanes])
+            before = zeros
+            for c in range(2 * blocks_in + 1):
+                if c < 2 * blocks_in:
+                    half = c % 2
+                    row = own32[c // 2 : c // 2 + 1, half * HALF : (half + 1) * HALF]
+                    now = pltpu.roll(
+                        jnp.broadcast_to(row, (HALF, HALF)), 1, 1, stride=1, stride_axis=0
+                    )
+                else:
+                    now = zeros
+                tile = jnp.where(below, before, now).astype(jnp.bfloat16)
+                before = now
+                chunk = c + lag_blocks - 1
+                s = chunk // 2
+                if chunk % 2:
+                    put(j, s, 0, 1, tile)
+                    put(j, s, 1, 0, tile)
+                else:
+                    put(j, s, 0, 0, tile)
+                    put(j, s - 1, 1, 1, tile)
+            return carry
+
+        lax.fori_loop(0, own_count, one, 0)
+
+    def correlate_window(k):
+        blk = blks[k]
+        for d in range(owners):
+            for i in range(capacity):
+                station = asked_ref[e, d, i]
+                slot = (d * capacity + i) * comps * blocks_in
+                station_rows = (
+                    blk[d, pl.ds(station * comps, comps)]
+                    .astype(jnp.float32)
+                    .reshape(comps * blocks_in, BLOCK)
+                )
+                for h in (0, 1):
+                    pool32[h, slot : slot + comps * blocks_in, :] = station_rows[
+                        :, h * HALF : (h + 1) * HALF
+                    ]
+        for m in range(blocks_in):
+            for h in (0, 1):
+                part = pool32[h, pl.ds(m, pool, stride=blocks_in), :].astype(jnp.bfloat16)
+                for q in range(lag_blocks):
+                    s = m + q
+                    if first_s <= s <= last_s:
+                        col = (s - first_s) * BLOCK + h * HALF
+                        row = (lag_blocks - 1 - q) * pool
+                        lhs[row : row + pool, col : col + HALF] = part
+
+        def one(j, carry):
+            term = jnp.dot(lhs[...], hankel[j], preferred_element_type=jnp.float32)
+            if k == 0:
+                acc[j] = term
+            else:
+                acc[j] += term
+            return carry
+
+        lax.fori_loop(0, own_count, one, 0)
+
+    for k in (1, 2, 3):
+        z_copy(k).start()
+    send_own(0)
+    for q in range(lag_blocks):
+        for s in range(first_s, last_s + 1):
+            if not 0 <= s - (lag_blocks - 1) + q < blocks_in:
+                col = (s - first_s) * BLOCK
+                lhs[q * pool : (q + 1) * pool, col : col + BLOCK] = jnp.zeros((pool, BLOCK), jnp.bfloat16)
+    for j in range(own_count):
+        put(j, first_s, 0, 0, zeros.astype(jnp.bfloat16))
+        put(j, last_s, 1, 1, zeros.astype(jnp.bfloat16))
+
+    build(0)
+    z_copy(1).wait_recv()
+    send_own(1)
+    forward_xy(0)
+    z_copy(2).wait_recv()
+    send_own(2)
+    forward_diag(0)
+    forward_xy(1)
+    wait_core(0)
+    correlate_window(0)
+    z_copy(3).wait_recv()
+    send_own(3)
+    forward_diag(1)
+    forward_xy(2)
+    build(1)
+    wait_core(1)
+    correlate_window(1)
+    forward_diag(2)
+    forward_xy(3)
+    build(2)
+    wait_core(2)
+    correlate_window(2)
+    forward_diag(3)
+    build(3)
+    wait_core(3)
+    correlate_window(3)
+    cc_ref[...] = acc[...]
+
+    for k in (1, 2, 3):
+        z_copy(k).wait_send()
+    for k in range(4):
+        plane_copy(k, FROM_X, e, ex).wait_send()
+        plane_copy(k, FROM_Y, e, ey).wait_send()
+        plane_copy(k, CORE_OWN, e, ec).wait_send()
+        plane_copy(k, DIAG_A, ex, ey).wait_send()
+        plane_copy(k, CORE_X, ex, ec).wait_send()
+        plane_copy(k, DIAG_B, ey, ex).wait_send()
+        plane_copy(k, CORE_Y, ey, ec).wait_send()
+        plane_copy(k, CORE_D, ed, ec).wait_send()
+
+
+def select_kernel(scale, own_count, comps, lag_blocks, counts_ref, partners_ref, codes_ref, cc_ref, out_ref):
+    t = lax.axis_index("tm")
+    pool = cc_ref.shape[1] // lag_blocks
+    slots = partners_ref.shape[2]
+    pool_row = lax.broadcasted_iota(jnp.int32, (pool, slots), 0)
+    slot_lane = lax.broadcasted_iota(jnp.int32, (pool, slots), 1)
+    dims = (((0,), (0,)), ((), ()))
+    for j in range(own_count):
+        trace = own_count * t + j
+        wanted = partners_ref[0, pl.ds(trace, 1), :] * comps + codes_ref[0, pl.ds(trace, 1), :]
+        hit = (wanted == pool_row) & (slot_lane < counts_ref[0, trace])
+        chosen = jnp.where(hit, 1.0, 0.0).astype(jnp.bfloat16)
+        for q in range(lag_blocks):
+            part = cc_ref[j, q * pool : (q + 1) * pool, :]
+            high = part.astype(jnp.bfloat16)
+            rest = part - high.astype(jnp.float32)
+            middle = rest.astype(jnp.bfloat16)
+            low = (rest - middle.astype(jnp.float32)).astype(jnp.bfloat16)
+            total = lax.dot_general(chosen, low, dims, preferred_element_type=jnp.float32)
+            total += lax.dot_general(chosen, middle, dims, preferred_element_type=jnp.float32)
+            total += lax.dot_general(chosen, high, dims, preferred_element_type=jnp.float32)
+            lag = (lag_blocks - 1 - q) * BLOCK
+            out_ref[0, j * slots : (j + 1) * slots, lag : lag + BLOCK] = total * scale
+
+
+def gathered_shards(record, requested, partners, codes, counts):
+    stations, comps, _, window_len = record.shape
+    owners, capacity = requested.shape[1:]
+    traces = stations * comps
+    windows = lax.axis_size("tm")
+    own_count = traces // windows
+    blocks_in, lag_blocks = window_len // BLOCK, LAGS // BLOCK
+    pool = owners * capacity * comps
+    depth = (blocks_in + lag_blocks - 3) * BLOCK
+    slots = partners.shape[2]
+    cc_shape = jax.ShapeDtypeStruct((own_count, lag_blocks * pool, BLOCK), jnp.float32)
+    dims = (traces, blocks_in, owners, capacity, comps, own_count, lag_blocks)
+    vmem = pl.BlockSpec(memory_space=pltpu.VMEM)
+    smem = pl.BlockSpec(memory_space=pltpu.SMEM)
+    cc = pl.pallas_call(
+        functools.partial(exchange_kernel, dims),
+        out_shape=cc_shape,
+        in_specs=[smem, vmem],
+        out_specs=vmem,
+        scratch_shapes=[pltpu.VMEM((owners, traces, blocks_in, BLOCK), jnp.bfloat16)] * 4
+        + [
+            pltpu.VMEM((2, traces * blocks_in, HALF), jnp.float32),
+            pltpu.VMEM((2, pool * blocks_in, HALF), jnp.float32),
+            pltpu.VMEM((blocks_in, BLOCK), jnp.float32),
+            pltpu.VMEM((lag_blocks * pool, depth), jnp.bfloat16),
+            pltpu.VMEM((own_count, depth, BLOCK), jnp.bfloat16),
+            pltpu.VMEM(cc_shape.shape, jnp.float32),
+            pltpu.SemaphoreType.DMA((4, 8)),
+            pltpu.SemaphoreType.DMA((4, 8)),
+            pltpu.SemaphoreType.DMA((3,)),
+            pltpu.SemaphoreType.DMA((3,)),
+        ],
+        compiler_params=pltpu.CompilerParams(
+            collective_id=0, has_side_effects=True, vmem_limit_bytes=40 * 1024 * 1024
+        ),
+    )(requested, record.reshape(traces, window_len))
+    return pl.pallas_call(
+        functools.partial(
+            select_kernel, 1.0 / math.sqrt(window_len * windows), own_count, comps, lag_blocks
+        ),
+        out_shape=jax.ShapeDtypeStruct((1, own_count * slots, LAGS), jnp.float32),
+        in_specs=[smem, vmem, vmem, vmem],
+        out_specs=vmem,
+        compiler_params=pltpu.CompilerParams(vmem_limit_bytes=16 * 1024 * 1024),
+    )(counts, partners, codes, cc)
+
+
 def solution(mesh):
+    def body(record, requested, partners, codes, counts):
+        planes = lax.axis_size("tm") == 4 and lax.axis_size("pairs") == 8
+        stations, comps, window_count, window_len = record.shape
+        fits = (
+            window_count == 1
+            and stations == 4
+            and window_len % BLOCK == 0
+            and LAGS == 4 * BLOCK
+        )
+        form = gathered_shards if planes and fits else shards
+        return form(record, requested, partners, codes, counts)
+
     return jax.shard_map(
-        shards,
+        body,
         mesh=mesh,
         in_specs=(
             P("pairs", None, "tm", None),

time: 219 us -> 38.1 us (0.17)
  local copies, waits for them, and re-layouts: 85.1 us -> 2.6 us
  waiting for transfers between devices: 48.5 us -> 0 us
  matrix products: 44.5 us -> 0 us
  Pallas kernels: 0 us -> 35.1 us
  between operations: 13.5 us -> 0.03 us
  other arithmetic: 12.8 us -> 0 us
  blocking collectives: 12.4 us -> 0 us
    reduce_scatter x1 -> x0, waiting for transfers between devices: 48.5 us -> none  [shards(): return lax.psum_scatter(window_term, 'tm', scatter_dimension=1, tiled=True)]
    dot_general x96 -> x0, matrix products: 44.5 us -> none  [correlate(): jnp.einsum('pmi,imr->pr', pieces, window_view, preferred_element_type=jnp...]
    reshape x26 -> x1, local copies, waits for them, and re-layouts: 43.3 us -> 0.09 us  [gathered_shards(): record.reshape(traces, window_len)]
    pallas_call x0 -> x2, Pallas kernels: none -> 35.1 us  [the longest x1 33.3 us: gathered_shards(): pl.pallas_call(functools.partial(exchange_kernel, dims), out_shape=cc_sha...]
    while x24 -> x0, local copies, waits for them, and re-layouts: 13.1 us -> none
    all_gather x1 -> x0, blocking collectives: 12.4 us -> none  [shards(): everyone = lax.all_gather(whitened, 'pairs', axis=0, tiled=True)]
    slice x24 -> x0, local copies, waits for them, and re-layouts: 10.8 us -> none  [correlate(): skewed = spread.reshape(block_len, length + 1)[:, :window_len + lag_count]]
    dynamic_update_slice x12 -> x0, local copies, waits for them, and re-layouts: 8.4 us -> none  [shards(): lagged = lax.map(one_trace, (own_rows, picked))]
  transfers between devices with their start and end apart: 1 -> 0, of which waited for: 1 -> 0; matrix products, arithmetic and copies ran while one was open for 0% -> 0% of each run, Pallas kernels for 0% -> 0%
where the time goes in v1:
time: 38.1 us; the launch traced here: 37.8 us
  Pallas kernels  35.1 us (92%)
  local copies, waits for them, and re-layouts  2.6 us (7%)
    pallas_call x1, Pallas kernels, gathered_shards(): pl.pallas_call(functools.partial(exchange_kernel, dims), out_shape=cc_sha...  33.3 us
    unnamed x10, local copies, waits for them, and re-layouts  2.51 us
    pallas_call x1, Pallas kernels, gathered_shards(): pl.pallas_call(functools.partial(select_kernel, 1.0 / math.sqrt(window_le...  1.79 us

profile of v1, /device:TPU:0, one launch (start us, length us, event | category | flops | bytes accessed | tf_op | source)
XLA Modules:
  0.0 37.8 jit_solution(13228741393834555286)
XLA Ops:
  0.0 0.0 copy-start.2
  0.0 0.7 %copy.12.partners_ref = s32[1,12,48]{2,1,0:T(8,128)S(1)} copy(s32[1,12,48]{2,0,1:T(1,128)} %param.7) | data formatting | bytes 4608 | tf_op args[2]
  0.7 0.0 copy-done.2
  0.7 0.0 copy-start.1
  0.7 0.7 %copy-done.1 = s32[8,8,2]{1,2,0:T(2,128)S(1)} copy-done((s32[8,8,2]{1,2,0:T(2,128)S(1)}, s32[8,8,2]{1,2,0:T(2,128)}, u32[]{:S(2)}) %copy-start.1) | copy-done | bytes 536
  1.4 0.1 copy.11.asked_ref
  1.5 1.0 %copy.10 = bf16[4,3,1,4096]{3,1,0,2:T(4,128)(2,1)S(1)} copy(bf16[4,3,1,4096]{3,0,2,1:T(4,128)(2,1)} %param.5) | data formatting | bytes 196608 | tf_op args[0]
  2.5 0.1 reshape.3.record_ref
  2.6 0.0 copy-start
  2.6 33.3 %shard_map.55.cc_ref = f32[3,192,256]{2,1,0:T(8,128)S(1)} custom-call(s32[8,8,2]{2,1,0:T(8,128)S(1)} %copy.11.asked_ref, bf16[12,4096]{1,0:T(8,128)(2,1)S(1)} %reshape.3.record_ref), custom_call_target="tpu_custom_call" | custom-call | tf_op jit(solution)/shard_map/pallas_call | solution.py:345
  36.0 0.0 copy-done
  36.0 1.8 %shard_map.56 = f32[1,144,1024]{2,1,0:T(8,128)} custom-call(s32[1,12]{1,0:T(1,128)S(1)} %copy-done, s32[1,12,48]{2,1,0:T(8,128)S(1)} %copy.12.partners_ref, s32[1,12,48]{2,1,0:T(8,128)S(1)} %copy.13.codes_ref, f32[3,192,256]{2,1,0:T(8,128)S(1)} %shard_map.55.cc_ref), custom_call_target="tpu_custom_call" | custom-call | tf_op jit(solution)/shard_map/pallas_call | solution.py:367
  (1 shorter events, 0.0 us)
Async XLA Ops:
  0.0 0.7 %copy-start.2 = (s32[1,12,48]{2,0,1:T(1,128)S(1)}, s32[1,12,48]{2,0,1:T(1,128)}, u32[]{:S(2)}) copy-start(s32[1,12,48]{2,0,1:T(1,128)} %param.8) | copy-start | bytes 6916
  0.7 0.7 %copy-start.1 = (s32[8,8,2]{1,2,0:T(2,128)S(1)}, s32[8,8,2]{1,2,0:T(2,128)}, u32[]{:S(2)}) copy-start(s32[8,8,2]{1,2,0:T(2,128)} %param.6) | copy-start | bytes 1540
  2.6 33.4 %copy-start = (s32[1,12]{1,0:T(1,128)S(1)}, s32[1,12]{1,0:T(1,128)}, u32[]{:S(2)}) copy-start(s32[1,12]{1,0:T(1,128)} %counts_ref.1) | copy-start | bytes 148

commit v2 on v1

--- a/solution.py
+++ b/solution.py
@@ -96,7 +96,7 @@
 ):
     traces, blocks_in, owners, capacity, comps, own_count, lag_blocks = dims
     blks = scratch[:4]
-    (rows32, pool32, own32, lhs, hankel, acc, send, recv, zsend, zrecv) = scratch[4:]
+    (rows32, pool32, own32, pool16, hankel, send, recv, zsend, zrecv) = scratch[4:]
     pool = owners * capacity * comps
     first_s, last_s = 1, blocks_in + lag_blocks - 3
     t = lax.axis_index("tm")
@@ -117,14 +117,17 @@
     def flip_halves(tile):
         return jnp.dot(tile, mirror, preferred_element_type=jnp.float32)
 
-    values = record_ref[...].astype(jnp.float32)
-    values = values - jnp.mean(values, axis=-1, keepdims=True)
-    power_mean = jnp.mean(values * values, axis=-1, keepdims=True)
-    values = values * lax.rsqrt(power_mean + 1e-06)
-    for m in range(blocks_in):
-        for h in (0, 1):
-            lane = m * BLOCK + h * HALF
-            rows32[h, pl.ds(m, traces, stride=blocks_in), :] = values[:, lane : lane + HALF]
+    stations = traces // comps
+    for comp in range(comps):
+        values = record_ref[comp].astype(jnp.float32)
+        values = values - jnp.mean(values, axis=-1, keepdims=True)
+        power_mean = jnp.mean(values * values, axis=-1, keepdims=True)
+        values = values * lax.rsqrt(power_mean + 1e-06)
+        for m in range(blocks_in):
+            rows = pl.ds(comp * blocks_in + m, stations, stride=comps * blocks_in)
+            for h in (0, 1):
+                lane = m * BLOCK + h * HALF
+                rows32[h, rows, :] = values[:, lane : lane + HALF]
     for h in (0, 1):
         blks[0][e, :, :, h * HALF : (h + 1) * HALF] = (
             flip_halves(rows32[h].astype(jnp.bfloat16))
@@ -179,38 +182,33 @@
         plane_copy(k, CORE_D, cd, ec).wait_recv()
 
     below = lane_index <= row_index
-    zeros = jnp.zeros((HALF, HALF), jnp.float32)
-
-    def put(j, s, row_half, lane_half, tile):
-        if first_s <= s <= last_s:
-            row = (s - first_s) * BLOCK + row_half * HALF
-            hankel[j, row : row + HALF, lane_half * HALF : (lane_half + 1) * HALF] = tile
+    nothing = jnp.zeros((HALF, HALF), jnp.bfloat16)
+    first_chunk = 2 * first_s
+
+    def put(k, j, chunk, tile):
+        lane = (chunk - first_chunk) * HALF
+        hankel[own_count * k + j, :, lane : lane + HALF] = tile
 
     def build(k):
         def one(j, carry):
             for h in (0, 1):
                 lanes = slice(h * HALF, (h + 1) * HALF)
                 own32[:, lanes] = flip_halves(blks[k][e, own_count * t + j, :, lanes])
-            before = zeros
+            before = nothing
             for c in range(2 * blocks_in + 1):
                 if c < 2 * blocks_in:
                     half = c % 2
                     row = own32[c // 2 : c // 2 + 1, half * HALF : (half + 1) * HALF]
-                    now = pltpu.roll(
-                        jnp.broadcast_to(row, (HALF, HALF)), 1, 1, stride=1, stride_axis=0
+                    skewed = pltpu.roll(
+                        jnp.broadcast_to(row, (16, HALF)), 1, 1, stride=1, stride_axis=0
+                    ).astype(jnp.bfloat16)
+                    now = jnp.concatenate(
+                        [skewed] + [pltpu.roll(skewed, 16 * a, 1) for a in range(1, HALF // 16)], axis=0
                     )
                 else:
-                    now = zeros
-                tile = jnp.where(below, before, now).astype(jnp.bfloat16)
+                    now = nothing
+                put(k, j, c + lag_blocks - 1, jnp.where(below, before, now))
                 before = now
-                chunk = c + lag_blocks - 1
-                s = chunk // 2
-                if chunk % 2:
-                    put(j, s, 0, 1, tile)
-                    put(j, s, 1, 0, tile)
-                else:
-                    put(j, s, 0, 0, tile)
-                    put(j, s - 1, 1, 1, tile)
             return carry
 
         lax.fori_loop(0, own_count, one, 0)
@@ -219,7 +217,7 @@
         blk = blks[k]
         for d in range(owners):
             for i in range(capacity):
-                station = asked_ref[e, d, i]
+                station = asked_ref[e, i, d]
                 slot = (d * capacity + i) * comps * blocks_in
                 station_rows = (
                     blk[d, pl.ds(station * comps, comps)]
@@ -233,19 +231,37 @@
         for m in range(blocks_in):
             for h in (0, 1):
                 part = pool32[h, pl.ds(m, pool, stride=blocks_in), :].astype(jnp.bfloat16)
-                for q in range(lag_blocks):
-                    s = m + q
-                    if first_s <= s <= last_s:
-                        col = (s - first_s) * BLOCK + h * HALF
-                        row = (lag_blocks - 1 - q) * pool
-                        lhs[row : row + pool, col : col + HALF] = part
+                pool16[m, :, h * HALF : (h + 1) * HALF] = part
 
         def one(j, carry):
-            term = jnp.dot(lhs[...], hankel[j], preferred_element_type=jnp.float32)
+            empty = jnp.zeros((pool, BLOCK), jnp.bfloat16)
+            left = jnp.concatenate(
+                [
+                    jnp.concatenate(
+                        [
+                            pool16[s - q] if 0 <= s - q < blocks_in else empty
+                            for s in range(first_s, last_s + 1)
+                        ],
+                        axis=1,
+                    )
+                    for q in reversed(range(lag_blocks))
+                ],
+                axis=0,
+            )
+            index = own_count * k + j
+            right = jnp.concatenate(
+                [
+                    hankel[index, :, lane : lane + BLOCK]
+                    for s in range(first_s, last_s + 1)
+                    for lane in ((2 * s - first_chunk) * HALF, (2 * s + 1 - first_chunk) * HALF)
+                ],
+                axis=0,
+            )
+            term = jnp.dot(left, right, preferred_element_type=jnp.float32)
             if k == 0:
-                acc[j] = term
+                cc_ref[j] = term
             else:
-                acc[j] += term
+                cc_ref[j] += term
             return carry
 
         lax.fori_loop(0, own_count, one, 0)
@@ -253,42 +269,37 @@
     for k in (1, 2, 3):
         z_copy(k).start()
     send_own(0)
-    for q in range(lag_blocks):
-        for s in range(first_s, last_s + 1):
-            if not 0 <= s - (lag_blocks - 1) + q < blocks_in:
-                col = (s - first_s) * BLOCK
-                lhs[q * pool : (q + 1) * pool, col : col + BLOCK] = jnp.zeros((pool, BLOCK), jnp.bfloat16)
-    for j in range(own_count):
-        put(j, first_s, 0, 0, zeros.astype(jnp.bfloat16))
-        put(j, last_s, 1, 1, zeros.astype(jnp.bfloat16))
+    for k in range(4):
+        for j in range(own_count):
+            put(k, j, first_chunk, nothing)
+            put(k, j, 2 * last_s + 2, nothing)
 
     build(0)
     z_copy(1).wait_recv()
     send_own(1)
+    build(1)
     forward_xy(0)
     z_copy(2).wait_recv()
     send_own(2)
+    build(2)
     forward_diag(0)
     forward_xy(1)
+    z_copy(3).wait_recv()
+    send_own(3)
     wait_core(0)
     correlate_window(0)
-    z_copy(3).wait_recv()
-    send_own(3)
     forward_diag(1)
     forward_xy(2)
-    build(1)
+    build(3)
     wait_core(1)
     correlate_window(1)
     forward_diag(2)
     forward_xy(3)
-    build(2)
     wait_core(2)
     correlate_window(2)
     forward_diag(3)
-    build(3)
     wait_core(3)
     correlate_window(3)
-    cc_ref[...] = acc[...]
 
     for k in (1, 2, 3):
         z_copy(k).wait_send()
@@ -312,7 +323,7 @@
     dims = (((0,), (0,)), ((), ()))
     for j in range(own_count):
         trace = own_count * t + j
-        wanted = partners_ref[0, pl.ds(trace, 1), :] * comps + codes_ref[0, pl.ds(trace, 1), :]
+        wanted = partners_ref[trace] * comps + codes_ref[trace]
         hit = (wanted == pool_row) & (slot_lane < counts_ref[0, trace])
         chosen = jnp.where(hit, 1.0, 0.0).astype(jnp.bfloat16)
         for q in range(lag_blocks):
@@ -352,9 +363,8 @@
             pltpu.VMEM((2, traces * blocks_in, HALF), jnp.float32),
             pltpu.VMEM((2, pool * blocks_in, HALF), jnp.float32),
             pltpu.VMEM((blocks_in, BLOCK), jnp.float32),
-            pltpu.VMEM((lag_blocks * pool, depth), jnp.bfloat16),
-            pltpu.VMEM((own_count, depth, BLOCK), jnp.bfloat16),
-            pltpu.VMEM(cc_shape.shape, jnp.float32),
+            pltpu.VMEM((blocks_in, pool, BLOCK), jnp.bfloat16),
+            pltpu.VMEM((4 * own_count, HALF, depth + HALF), jnp.bfloat16),
             pltpu.SemaphoreType.DMA((4, 8)),
             pltpu.SemaphoreType.DMA((4, 8)),
             pltpu.SemaphoreType.DMA((3,)),
@@ -363,7 +373,7 @@
         compiler_params=pltpu.CompilerParams(
             collective_id=0, has_side_effects=True, vmem_limit_bytes=40 * 1024 * 1024
         ),
-    )(requested, record.reshape(traces, window_len))
+    )(requested.transpose(0, 2, 1), record.transpose(2, 1, 0, 3)[0])
     return pl.pallas_call(
         functools.partial(
             select_kernel, 1.0 / math.sqrt(window_len * windows), own_count, comps, lag_blocks
@@ -372,7 +382,7 @@
         in_specs=[smem, vmem, vmem, vmem],
         out_specs=vmem,
         compiler_params=pltpu.CompilerParams(vmem_limit_bytes=16 * 1024 * 1024),
-    )(counts, partners, codes, cc)
+    )(counts, partners.transpose(1, 0, 2), codes.transpose(1, 0, 2), cc)
 
 
 def solution(mesh):

time: 38.1 us -> 35.1 us (0.921)
  Pallas kernels: 35.1 us -> 33.2 us
  local copies, waits for them, and re-layouts: 2.6 us -> 1.6 us
    pallas_call x1, Pallas kernels: 33.3 us -> 31.4 us  [gathered_shards(): pl.pallas_call(functools.partial(exchange_kernel, dims), out_shape=cc_sha...]
    unnamed x10, local copies, waits for them, and re-layouts: 2.51 us -> 1.6 us
where the time goes in v2:
time: 35.1 us; the launch traced here: 34.9 us
  Pallas kernels  33.2 us (95%)
  local copies, waits for them, and re-layouts  1.6 us (5%)
    pallas_call x1, Pallas kernels, gathered_shards(): pl.pallas_call(functools.partial(exchange_kernel, dims), out_shape=cc_sha...  31.4 us
    pallas_call x1, Pallas kernels, gathered_shards(): pl.pallas_call(functools.partial(select_kernel, 1.0 / math.sqrt(window_le...  1.79 us
    unnamed x10, local copies, waits for them, and re-layouts  1.6 us

profile of v2, /device:TPU:0, one launch (start us, length us, event | category | flops | bytes accessed | tf_op | source)
XLA Modules:
  0.0 34.9 jit_solution(3078586097759108464)
XLA Ops:
  0.0 0.0 copy-start
  0.0 0.9 %copy-done = bf16[4,3,1,4096]{3,0,2,1:T(4,128)(2,1)S(1)} copy-done((bf16[4,3,1,4096]{3,0,2,1:T(4,128)(2,1)S(1)}, bf16[4,3,1,4096]{3,0,2,1:T(4,128)(2,1)}, u32[]{:S(2)}) %copy-start) | copy-done | bytes 98328
  0.9 0.0 copy-start.1
  0.9 0.7 %copy-done.1 = s32[8,8,2]{1,2,0:T(2,128)S(1)} copy-done((s32[8,8,2]{1,2,0:T(2,128)S(1)}, s32[8,8,2]{1,2,0:T(2,128)}, u32[]{:S(2)}) %copy-start.1) | copy-done | bytes 536
  1.6 0.0 copy-start.2
  1.6 0.0 copy-start.3
  1.6 0.0 copy-start.4
  1.6 31.4 %shard_map.55.cc_ref = f32[3,192,256]{2,1,0:T(8,128)S(1)} custom-call(s32[8,2,8]{2,1,0:T(2,128)S(1)} %bitcast.9, bf16[3,4,4096]{2,1,0:T(4,128)(2,1)S(1)} %bitcast.8), custom_call_target="tpu_custom_call" | custom-call | tf_op jit(solution)/shard_map/pallas_call | solution.py:356
  33.0 0.0 copy-done.2
  33.0 0.0 copy-done.3
  33.1 0.0 copy-done.4
  33.1 1.8 %shard_map.56 = f32[1,144,1024]{2,1,0:T(8,128)} custom-call(s32[1,12]{1,0:T(1,128)S(1)} %copy-done.4, s32[12,1,48]{2,1,0:T(1,128)S(1)} %bitcast.10, s32[12,1,48]{2,1,0:T(1,128)S(1)} %bitcast.11, f32[3,192,256]{2,1,0:T(8,128)S(1)} %shard_map.55.cc_ref), custom_call_target="tpu_custom_call" | custom-call | tf_op jit(solution)/shard_map/pallas_call | solution.py:377
Async XLA Ops:
  0.0 0.9 %copy-start = (bf16[4,3,1,4096]{3,0,2,1:T(4,128)(2,1)S(1)}, bf16[4,3,1,4096]{3,0,2,1:T(4,128)(2,1)}, u32[]{:S(2)}) copy-start(bf16[4,3,1,4096]{3,0,2,1:T(4,128)(2,1)} %param.5) | copy-start | bytes 294916
  0.9 0.7 %copy-start.1 = (s32[8,8,2]{1,2,0:T(2,128)S(1)}, s32[8,8,2]{1,2,0:T(2,128)}, u32[]{:S(2)}) copy-start(s32[8,8,2]{1,2,0:T(2,128)} %param.6) | copy-start | bytes 1540
  1.6 31.4 %copy-start.2 = (s32[1,12,48]{2,0,1:T(1,128)S(1)}, s32[1,12,48]{2,0,1:T(1,128)}, u32[]{:S(2)}) copy-start(s32[1,12,48]{2,0,1:T(1,128)} %param.7) | copy-start | bytes 6916
  1.6 31.5 %copy-start.3 = (s32[1,12,48]{2,0,1:T(1,128)S(1)}, s32[1,12,48]{2,0,1:T(1,128)}, u32[]{:S(2)}) copy-start(s32[1,12,48]{2,0,1:T(1,128)} %param.8) | copy-start | bytes 6916
  1.6 31.5 %copy-start.4 = (s32[1,12]{1,0:T(1,128)S(1)}, s32[1,12]{1,0:T(1,128)}, u32[]{:S(2)}) copy-start(s32[1,12]{1,0:T(1,128)} %counts_ref.1) | copy-start | bytes 148

commit v3 on v2

--- a/solution.py
+++ b/solution.py
@@ -83,20 +83,13 @@
 FROM_X, FROM_Y, DIAG_A, DIAG_B, CORE_OWN, CORE_X, CORE_Y, CORE_D = range(8)
 
 
-def xor_step(t, k):
-    if k == 1:
-        return t + 1 - 2 * lax.rem(t, 2)
-    if k == 2:
-        return lax.rem(t + 2, 4)
-    return 3 - t
-
-
 def exchange_kernel(
-    dims, asked_ref, record_ref, cc_ref, *scratch
+    dims, asked_hbm, record_hbm, cc_ref, *scratch
 ):
     traces, blocks_in, owners, capacity, comps, own_count, lag_blocks = dims
     blks = scratch[:4]
-    (rows32, pool32, own32, pool16, hankel, send, recv, zsend, zrecv) = scratch[4:]
+    (asked_ref, record_ref, rows32, pool32, own32, pool16, hankel) = scratch[4:11]
+    (send, recv, zsend, zrecv, local) = scratch[11:]
     pool = owners * capacity * comps
     first_s, last_s = 1, blocks_in + lag_blocks - 3
     t = lax.axis_index("tm")
@@ -106,8 +99,15 @@
     ed = ex + 4 - 8 * y
     cx, cy, cd = ex + 1 - 2 * core, ey + 1 - 2 * core, ed + 1 - 2 * core
 
+    near, far = t + 1 - 2 * lax.rem(t, 2), 3 - t
+    inner = (t == 1) | (t == 2)
+
+    load_asked = pltpu.make_async_copy(asked_hbm, asked_ref, local.at[0])
+    load_record = pltpu.make_async_copy(record_hbm, record_ref, local.at[1])
+    load_record.start()
+    load_asked.start()
     barrier = pltpu.get_barrier_semaphore()
-    for peer in ((t, ex), (t, ey), (t, ec)) + tuple((xor_step(t, k), e) for k in (1, 2, 3)):
+    for peer in ((t, ex), (t, ey), (t, ec), (near, e), (far, e)):
         pl.semaphore_signal(barrier, inc=1, device_id=peer, device_id_type=MESH)
 
     row_index = lax.broadcasted_iota(jnp.int32, (HALF, HALF), 0)
@@ -118,6 +118,7 @@
         return jnp.dot(tile, mirror, preferred_element_type=jnp.float32)
 
     stations = traces // comps
+    load_record.wait()
     for comp in range(comps):
         values = record_ref[comp].astype(jnp.float32)
         values = values - jnp.mean(values, axis=-1, keepdims=True)
@@ -134,7 +135,7 @@
             .astype(jnp.bfloat16)
             .reshape(traces, blocks_in, HALF)
         )
-    pl.semaphore_wait(barrier, 6)
+    pl.semaphore_wait(barrier, 5)
 
     def plane_copy(k, kind, origin, target):
         blk = blks[k]
@@ -150,12 +151,21 @@
             device_id=(t, target), device_id_type=MESH,
         )
 
-    def z_copy(k):
+    def z_copy(index, source, slot, target):
         return pltpu.make_async_remote_copy(
-            src_ref=blks[0].at[e], dst_ref=blks[k].at[e],
-            send_sem=zsend.at[k - 1], recv_sem=zrecv.at[k - 1],
-            device_id=(xor_step(t, k), e), device_id_type=MESH,
+            src_ref=blks[source].at[e], dst_ref=blks[slot].at[e],
+            send_sem=zsend.at[index], recv_sem=zrecv.at[slot - 1],
+            device_id=(target, e), device_id_type=MESH,
         )
+
+    own_near = z_copy(0, 0, 1, near)
+    own_far = z_copy(1, 0, 2, far)
+    near_to_far = z_copy(2, 1, 3, far)
+    far_to_near = z_copy(3, 2, 2, near)
+    rest_to_near = z_copy(4, 3, 3, near)
+
+    def wait_window(k):
+        z_copy(0, 0, k, near).wait_recv()
 
     def send_own(k):
         plane_copy(k, FROM_X, e, ex).start()
@@ -213,7 +223,7 @@
 
         lax.fori_loop(0, own_count, one, 0)
 
-    def correlate_window(k):
+    def correlate_window(k, between=lambda: None):
         blk = blks[k]
         for d in range(owners):
             for i in range(capacity):
@@ -264,10 +274,16 @@
                 cc_ref[j] += term
             return carry
 
-        lax.fori_loop(0, own_count, one, 0)
-
-    for k in (1, 2, 3):
-        z_copy(k).start()
+        lax.fori_loop(0, own_count - 1, one, 0)
+        between()
+        one(own_count - 1, 0)
+
+    own_near.start()
+
+    @pl.when(inner)
+    def _():
+        own_far.start()
+
     send_own(0)
     for k in range(4):
         for j in range(own_count):
@@ -275,34 +291,61 @@
             put(k, j, 2 * last_s + 2, nothing)
 
     build(0)
-    z_copy(1).wait_recv()
+    wait_window(1)
+
+    @pl.when(inner)
+    def _():
+        near_to_far.start()
+        wait_window(2)
+        far_to_near.start()
+
     send_own(1)
+    forward_xy(0)
     build(1)
-    forward_xy(0)
-    z_copy(2).wait_recv()
+    forward_diag(0)
+
+    @pl.when(jnp.logical_not(inner))
+    def _():
+        wait_window(2)
+
+    @pl.when(inner)
+    def _():
+        wait_window(3)
+        rest_to_near.start()
+
     send_own(2)
-    build(2)
-    forward_diag(0)
     forward_xy(1)
-    z_copy(3).wait_recv()
-    send_own(3)
+    load_asked.wait()
     wait_core(0)
     correlate_window(0)
     forward_diag(1)
+    build(2)
+
+    @pl.when(jnp.logical_not(inner))
+    def _():
+        wait_window(3)
+
+    send_own(3)
     forward_xy(2)
-    build(3)
     wait_core(1)
     correlate_window(1)
     forward_diag(2)
+    build(3)
     forward_xy(3)
     wait_core(2)
-    correlate_window(2)
-    forward_diag(3)
+    correlate_window(2, functools.partial(forward_diag, 3))
     wait_core(3)
     correlate_window(3)
 
-    for k in (1, 2, 3):
-        z_copy(k).wait_send()
+    own_near.wait_send()
+
+    @pl.when(inner)
+    def _():
+        own_far.wait_send()
+        near_to_far.wait_send()
+        far_to_near.wait_send()
+        rest_to_near.wait_send()
+
     for k in range(4):
         plane_copy(k, FROM_X, e, ex).wait_send()
         plane_copy(k, FROM_Y, e, ey).wait_send()
@@ -356,10 +399,12 @@
     cc = pl.pallas_call(
         functools.partial(exchange_kernel, dims),
         out_shape=cc_shape,
-        in_specs=[smem, vmem],
+        in_specs=[pl.BlockSpec(memory_space=pltpu.HBM)] * 2,
         out_specs=vmem,
         scratch_shapes=[pltpu.VMEM((owners, traces, blocks_in, BLOCK), jnp.bfloat16)] * 4
         + [
+            pltpu.SMEM((owners, capacity, owners), jnp.int32),
+            pltpu.VMEM((comps, stations, window_len), jnp.bfloat16),
             pltpu.VMEM((2, traces * blocks_in, HALF), jnp.float32),
             pltpu.VMEM((2, pool * blocks_in, HALF), jnp.float32),
             pltpu.VMEM((blocks_in, BLOCK), jnp.float32),
@@ -367,11 +412,12 @@
             pltpu.VMEM((4 * own_count, HALF, depth + HALF), jnp.bfloat16),
             pltpu.SemaphoreType.DMA((4, 8)),
             pltpu.SemaphoreType.DMA((4, 8)),
+            pltpu.SemaphoreType.DMA((5,)),
             pltpu.SemaphoreType.DMA((3,)),
-            pltpu.SemaphoreType.DMA((3,)),
+            pltpu.SemaphoreType.DMA((2,)),
         ],
         compiler_params=pltpu.CompilerParams(
-            collective_id=0, has_side_effects=True, vmem_limit_bytes=40 * 1024 * 1024
+            collective_id=0, has_side_effects=True, vmem_limit_bytes=60 * 1024 * 1024
         ),
     )(requested.transpose(0, 2, 1), record.transpose(2, 1, 0, 3)[0])
     return pl.pallas_call(

time: 35.1 us -> 35.7 us (1.017)
  Pallas kernels: 33.2 us -> 34.2 us
  local copies, waits for them, and re-layouts: 1.6 us -> 1.07 us
    pallas_call x1, Pallas kernels: 31.4 us -> 32.4 us  [gathered_shards(): pl.pallas_call(functools.partial(exchange_kernel, dims), out_shape=cc_sha...]
    unnamed x10 -> x8, local copies, waits for them, and re-layouts: 1.6 us -> 1.07 us
where the time goes in v3:
time: 35.7 us; the launch traced here: 35.3 us
  Pallas kernels  34.2 us (96%)
  local copies, waits for them, and re-layouts  1.07 us (3%)
    pallas_call x1, Pallas kernels, gathered_shards(): pl.pallas_call(functools.partial(exchange_kernel, dims), out_shape=cc_sha...  32.4 us
    pallas_call x1, Pallas kernels, gathered_shards(): pl.pallas_call(functools.partial(select_kernel, 1.0 / math.sqrt(window_le...  1.81 us
    unnamed x8, local copies, waits for them, and re-layouts  1.07 us

profile of v3, /device:TPU:0, one launch (start us, length us, event | category | flops | bytes accessed | tf_op | source)
XLA Modules:
  0.0 35.3 jit_solution(9294029572685999799)
XLA Ops:
  0.0 0.0 copy-start.1
  0.0 0.0 copy-start.2
  0.0 0.0 copy-start.3
  0.0 32.4 %shard_map.55.cc_ref = f32[3,192,256]{2,1,0:T(8,128)} custom-call(s32[8,2,8]{2,1,0:T(2,128)} %bitcast.11, bf16[3,4,4096]{2,1,0:T(4,128)(2,1)} %bitcast.10), custom_call_target="tpu_custom_call" | custom-call | tf_op jit(solution)/shard_map/pallas_call | solution.py:399
  32.4 0.0 copy-done.1
  32.4 0.0 copy-done.2
  32.5 0.0 copy-done.3
  32.5 0.0 copy-start
  32.5 1.1 %copy-done = f32[3,192,256]{2,1,0:T(8,128)S(1)} copy-done((f32[3,192,256]{2,1,0:T(8,128)S(1)}, f32[3,192,256]{2,1,0:T(8,128)}, u32[]{:S(2)}) %copy-start) | copy-done | bytes 589848
  33.5 1.8 %shard_map.56 = f32[1,144,1024]{2,1,0:T(8,128)} custom-call(s32[1,12]{1,0:T(1,128)S(1)} %copy-done.3, s32[12,1,48]{2,1,0:T(1,128)S(1)} %bitcast.8, s32[12,1,48]{2,1,0:T(1,128)S(1)} %bitcast.9, f32[3,192,256]{2,1,0:T(8,128)S(1)} %copy-done), custom_call_target="tpu_custom_call" | custom-call | tf_op jit(solution)/shard_map/pallas_call | solution.py:423
Async XLA Ops:
  0.0 32.4 %copy-start.1 = (s32[1,12,48]{2,0,1:T(1,128)S(1)}, s32[1,12,48]{2,0,1:T(1,128)}, u32[]{:S(2)}) copy-start(s32[1,12,48]{2,0,1:T(1,128)} %param.7) | copy-start | bytes 6916
  0.0 32.4 %copy-start.2 = (s32[1,12,48]{2,0,1:T(1,128)S(1)}, s32[1,12,48]{2,0,1:T(1,128)}, u32[]{:S(2)}) copy-start(s32[1,12,48]{2,0,1:T(1,128)} %param.8) | copy-start | bytes 6916
  0.0 32.5 %copy-start.3 = (s32[1,12]{1,0:T(1,128)S(1)}, s32[1,12]{1,0:T(1,128)}, u32[]{:S(2)}) copy-start(s32[1,12]{1,0:T(1,128)} %counts_ref.1) | copy-start | bytes 148
  32.5 1.1 %copy-start = (f32[3,192,256]{2,1,0:T(8,128)S(1)}, f32[3,192,256]{2,1,0:T(8,128)}, u32[]{:S(2)}) copy-start(f32[3,192,256]{2,1,0:T(8,128)} %shard_map.55.cc_ref) | copy-start | bytes 1769476

commit v4 on v3

--- a/solution.py
+++ b/solution.py
@@ -119,7 +119,8 @@
 
     stations = traces // comps
     load_record.wait()
-    for comp in range(comps):
+
+    def whiten(comp, carry):
         values = record_ref[comp].astype(jnp.float32)
         values = values - jnp.mean(values, axis=-1, keepdims=True)
         power_mean = jnp.mean(values * values, axis=-1, keepdims=True)
@@ -129,6 +130,9 @@
             for h in (0, 1):
                 lane = m * BLOCK + h * HALF
                 rows32[h, rows, :] = values[:, lane : lane + HALF]
+        return carry
+
+    lax.fori_loop(0, comps, whiten, 0)
     for h in (0, 1):
         blks[0][e, :, :, h * HALF : (h + 1) * HALF] = (
             flip_halves(rows32[h].astype(jnp.bfloat16))
@@ -195,49 +199,67 @@
     nothing = jnp.zeros((HALF, HALF), jnp.bfloat16)
     first_chunk = 2 * first_s
 
-    def put(k, j, chunk, tile):
-        lane = (chunk - first_chunk) * HALF
-        hankel[own_count * k + j, :, lane : lane + HALF] = tile
-
-    def build(k):
-        def one(j, carry):
+    last_chunk = 2 * last_s + 2
+
+    def unmirror(k):
+        for j in range(own_count):
             for h in (0, 1):
                 lanes = slice(h * HALF, (h + 1) * HALF)
-                own32[:, lanes] = flip_halves(blks[k][e, own_count * t + j, :, lanes])
-            before = nothing
-            for c in range(2 * blocks_in + 1):
-                if c < 2 * blocks_in:
-                    half = c % 2
-                    row = own32[c // 2 : c // 2 + 1, half * HALF : (half + 1) * HALF]
-                    skewed = pltpu.roll(
-                        jnp.broadcast_to(row, (16, HALF)), 1, 1, stride=1, stride_axis=0
-                    ).astype(jnp.bfloat16)
-                    now = jnp.concatenate(
-                        [skewed] + [pltpu.roll(skewed, 16 * a, 1) for a in range(1, HALF // 16)], axis=0
-                    )
-                else:
-                    now = nothing
-                put(k, j, c + lag_blocks - 1, jnp.where(below, before, now))
-                before = now
+                own32[j, :, lanes] = flip_halves(blks[k][e, own_count * t + j, :, lanes])
+
+    def build(n):
+        def one(j, carry):
+            index = own_count * n + j
+
+            def eight_blocks(g, before):
+                rows = own32[j, pl.ds(pl.multiple_of(8 * g, 8), 8), :]
+                for b in range(8):
+                    m = 8 * g + b
+                    for half in (0, 1):
+                        row = rows[b : b + 1, half * HALF : (half + 1) * HALF]
+                        skewed = pltpu.roll(
+                            jnp.broadcast_to(row, (16, HALF)), 1, 1, stride=1, stride_axis=0
+                        ).astype(jnp.bfloat16)
+                        now = jnp.concatenate(
+                            [skewed] + [pltpu.roll(skewed, 16 * a, 1) for a in range(1, HALF // 16)],
+                            axis=0,
+                        )
+                        lane = (2 * m + half + lag_blocks - 1 - first_chunk) * HALF
+                        hankel[index, :, pl.ds(pl.multiple_of(lane, HALF), HALF)] = jnp.where(
+                            below, before, now
+                        )
+                        before = now
+                return before
+
+            before = lax.fori_loop(0, blocks_in // 8, eight_blocks, nothing)
+            lane = (2 * blocks_in + lag_blocks - 1 - first_chunk) * HALF
+            hankel[index, :, lane : lane + HALF] = jnp.where(below, before, nothing)
+            hankel[index, :, :HALF] = nothing
+            lane = (last_chunk - first_chunk) * HALF
+            hankel[index, :, lane : lane + HALF] = nothing
             return carry
 
         lax.fori_loop(0, own_count, one, 0)
 
-    def correlate_window(k, between=lambda: None):
+    def pick(k):
         blk = blks[k]
-        for d in range(owners):
-            for i in range(capacity):
-                station = asked_ref[e, i, d]
-                slot = (d * capacity + i) * comps * blocks_in
-                station_rows = (
-                    blk[d, pl.ds(station * comps, comps)]
-                    .astype(jnp.float32)
-                    .reshape(comps * blocks_in, BLOCK)
-                )
-                for h in (0, 1):
-                    pool32[h, slot : slot + comps * blocks_in, :] = station_rows[
-                        :, h * HALF : (h + 1) * HALF
-                    ]
+
+        def one(slot, carry):
+            d, i = slot // capacity, lax.rem(slot, capacity)
+            station = asked_ref[e, i, d]
+            rows = (
+                blk[d, pl.ds(station * comps, comps)]
+                .astype(jnp.float32)
+                .reshape(comps * blocks_in, BLOCK)
+            )
+            start = pl.multiple_of(slot * (comps * blocks_in), comps * blocks_in)
+            for h in (0, 1):
+                pool32[h, pl.ds(start, comps * blocks_in), :] = rows[:, h * HALF : (h + 1) * HALF]
+            return carry
+
+        lax.fori_loop(0, owners * capacity, one, 0)
+
+    def correlate(n):
         for m in range(blocks_in):
             for h in (0, 1):
                 part = pool32[h, pl.ds(m, pool, stride=blocks_in), :].astype(jnp.bfloat16)
@@ -258,7 +280,7 @@
                 ],
                 axis=0,
             )
-            index = own_count * k + j
+            index = own_count * n + j
             right = jnp.concatenate(
                 [
                     hankel[index, :, lane : lane + BLOCK]
@@ -268,15 +290,22 @@
                 axis=0,
             )
             term = jnp.dot(left, right, preferred_element_type=jnp.float32)
-            if k == 0:
+
+            @pl.when(n == 0)
+            def _():
                 cc_ref[j] = term
-            else:
+
+            @pl.when(n > 0)
+            def _():
                 cc_ref[j] += term
+
+            @pl.when((n == 2) & (j == own_count - 2))
+            def _():
+                forward_diag(3)
+
             return carry
 
-        lax.fori_loop(0, own_count - 1, one, 0)
-        between()
-        one(own_count - 1, 0)
+        lax.fori_loop(0, own_count, one, 0)
 
     own_near.start()
 
@@ -285,57 +314,62 @@
         own_far.start()
 
     send_own(0)
-    for k in range(4):
-        for j in range(own_count):
-            put(k, j, first_chunk, nothing)
-            put(k, j, 2 * last_s + 2, nothing)
-
-    build(0)
-    wait_window(1)
-
-    @pl.when(inner)
-    def _():
-        near_to_far.start()
-        wait_window(2)
-        far_to_near.start()
-
-    send_own(1)
-    forward_xy(0)
-    build(1)
-    forward_diag(0)
-
-    @pl.when(jnp.logical_not(inner))
-    def _():
-        wait_window(2)
-
-    @pl.when(inner)
-    def _():
-        wait_window(3)
-        rest_to_near.start()
-
-    send_own(2)
-    forward_xy(1)
-    load_asked.wait()
-    wait_core(0)
-    correlate_window(0)
-    forward_diag(1)
-    build(2)
-
-    @pl.when(jnp.logical_not(inner))
-    def _():
-        wait_window(3)
-
-    send_own(3)
-    forward_xy(2)
-    wait_core(1)
-    correlate_window(1)
-    forward_diag(2)
-    build(3)
-    forward_xy(3)
-    wait_core(2)
-    correlate_window(2, functools.partial(forward_diag, 3))
-    wait_core(3)
-    correlate_window(3)
+    def before_build(n):
+        if n == 1:
+            wait_window(1)
+
+            @pl.when(inner)
+            def _():
+                near_to_far.start()
+                wait_window(2)
+                far_to_near.start()
+
+            send_own(1)
+            forward_xy(0)
+        if n == 2:
+            forward_diag(0)
+
+            @pl.when(jnp.logical_not(inner))
+            def _():
+                wait_window(2)
+
+            @pl.when(inner)
+            def _():
+                wait_window(3)
+                rest_to_near.start()
+
+            send_own(2)
+            forward_xy(1)
+            load_asked.wait()
+        if n == 3:
+            forward_diag(1)
+
+            @pl.when(jnp.logical_not(inner))
+            def _():
+                wait_window(3)
+
+            send_own(3)
+            forward_xy(2)
+        if n == 4:
+            forward_diag(2)
+            forward_xy(3)
+        if n < 4:
+            unmirror(n)
+
+    def before_correlate(n):
+        wait_core(n)
+        pick(n)
+
+    def step(n, carry):
+        for k in range(5):
+            pl.when(n == k)(functools.partial(before_build, k))
+        pl.when(n < 4)(functools.partial(build, n))
+        for k in range(4):
+            pl.when(n == k + 2)(functools.partial(before_correlate, k))
+        pl.when(n >= 2)(functools.partial(correlate, n - 2))
+        return carry
+
+    lax.fori_loop(0, 6, step, 0)
 
     own_near.wait_send()
 
@@ -358,28 +392,23 @@
 
 
 def select_kernel(scale, own_count, comps, lag_blocks, counts_ref, partners_ref, codes_ref, cc_ref, out_ref):
-    t = lax.axis_index("tm")
+    trace = own_count * lax.axis_index("tm") + pl.program_id(0)
     pool = cc_ref.shape[1] // lag_blocks
     slots = partners_ref.shape[2]
     pool_row = lax.broadcasted_iota(jnp.int32, (pool, slots), 0)
     slot_lane = lax.broadcasted_iota(jnp.int32, (pool, slots), 1)
     dims = (((0,), (0,)), ((), ()))
-    for j in range(own_count):
-        trace = own_count * t + j
-        wanted = partners_ref[trace] * comps + codes_ref[trace]
-        hit = (wanted == pool_row) & (slot_lane < counts_ref[0, trace])
-        chosen = jnp.where(hit, 1.0, 0.0).astype(jnp.bfloat16)
-        for q in range(lag_blocks):
-            part = cc_ref[j, q * pool : (q + 1) * pool, :]
-            high = part.astype(jnp.bfloat16)
-            rest = part - high.astype(jnp.float32)
-            middle = rest.astype(jnp.bfloat16)
-            low = (rest - middle.astype(jnp.float32)).astype(jnp.bfloat16)
-            total = lax.dot_general(chosen, low, dims, preferred_element_type=jnp.float32)
-            total += lax.dot_general(chosen, middle, dims, preferred_element_type=jnp.float32)
-            total += lax.dot_general(chosen, high, dims, preferred_element_type=jnp.float32)
-            lag = (lag_blocks - 1 - q) * BLOCK
-            out_ref[0, j * slots : (j + 1) * slots, lag : lag + BLOCK] = total * scale
+    wanted = partners_ref[trace] * comps + codes_ref[trace]
+    hit = (wanted == pool_row) & (slot_lane < counts_ref[0, trace])
+    chosen = jnp.where(hit, 1.0, 0.0).astype(jnp.bfloat16)
+    for q in range(lag_blocks):
+        part = cc_ref[0, q * pool : (q + 1) * pool, :]
+        high = part.astype(jnp.bfloat16)
+        low = (part - high.astype(jnp.float32)).astype(jnp.bfloat16)
+        total = lax.dot_general(chosen, low, dims, preferred_element_type=jnp.float32)
+        total += lax.dot_general(chosen, high, dims, preferred_element_type=jnp.float32)
+        lag = (lag_blocks - 1 - q) * BLOCK
+        out_ref[0, :, lag : lag + BLOCK] = total * scale
 
 
 def gathered_shards(record, requested, partners, codes, counts):
@@ -407,7 +436,7 @@
             pltpu.VMEM((comps, stations, window_len), jnp.bfloat16),
             pltpu.VMEM((2, traces * blocks_in, HALF), jnp.float32),
             pltpu.VMEM((2, pool * blocks_in, HALF), jnp.float32),
-            pltpu.VMEM((blocks_in, BLOCK), jnp.float32),
+            pltpu.VMEM((own_count, blocks_in, BLOCK), jnp.float32),
             pltpu.VMEM((blocks_in, pool, BLOCK), jnp.bfloat16),
             pltpu.VMEM((4 * own_count, HALF, depth + HALF), jnp.bfloat16),
             pltpu.SemaphoreType.DMA((4, 8)),
@@ -425,9 +454,10 @@
             select_kernel, 1.0 / math.sqrt(window_len * windows), own_count, comps, lag_blocks
         ),
         out_shape=jax.ShapeDtypeStruct((1, own_count * slots, LAGS), jnp.float32),
-        in_specs=[smem, vmem, vmem, vmem],
-        out_specs=vmem,
-        compiler_params=pltpu.CompilerParams(vmem_limit_bytes=16 * 1024 * 1024),
+        grid=(own_count,),
+        in_specs=[smem, vmem, vmem, pl.BlockSpec((1, lag_blocks * pool, BLOCK), lambda j: (j, 0, 0))],
+        out_specs=pl.BlockSpec((1, slots, LAGS), lambda j: (0, j, 0)),
+        compiler_params=pltpu.CompilerParams(vmem_limit_bytes=60 * 1024 * 1024),
     )(counts, partners.transpose(1, 0, 2), codes.transpose(1, 0, 2), cc)
 
 
@@ -438,7 +468,7 @@
         fits = (
             window_count == 1
             and stations == 4
-            and window_len % BLOCK == 0
+            and window_len % (8 * BLOCK) == 0
             and LAGS == 4 * BLOCK
         )
         form = gathered_shards if planes and fits else shards

time: 35.7 us -> 33 us (0.924)
  Pallas kernels: 34.2 us -> 32.7 us
  local copies, waits for them, and re-layouts: 1.07 us -> 0 us
    pallas_call x1, Pallas kernels: 32.4 us -> 29.6 us  [gathered_shards(): pl.pallas_call(functools.partial(exchange_kernel, dims), out_shape=cc_sha...]
    pallas_call x1, Pallas kernels: 1.81 us -> 3.15 us  [gathered_shards(): pl.pallas_call(functools.partial(select_kernel, 1.0 / math.sqrt(window_le...]
    unnamed x8 -> x0, local copies, waits for them, and re-layouts: 1.07 us -> none
where the time goes in v4:
time: 33 us; the launch traced here: 32.7 us
  Pallas kernels  32.7 us (99%)
    pallas_call x1, Pallas kernels, gathered_shards(): pl.pallas_call(functools.partial(exchange_kernel, dims), out_shape=cc_sha...  29.6 us
    pallas_call x1, Pallas kernels, gathered_shards(): pl.pallas_call(functools.partial(select_kernel, 1.0 / math.sqrt(window_le...  3.15 us

profile of v4, /device:TPU:0, one launch (start us, length us, event | category | flops | bytes accessed | tf_op | source)
XLA Modules:
  0.0 32.7 jit_solution(6711267040991411698)
XLA Ops:
  0.0 29.6 %shard_map.55.cc_ref = f32[3,192,256]{2,1,0:T(8,128)} custom-call(s32[8,2,8]{2,1,0:T(2,128)} %bitcast.9, bf16[3,4,4096]{2,1,0:T(4,128)(2,1)} %bitcast.8), custom_call_target="tpu_custom_call" | custom-call | tf_op jit(solution)/shard_map/pallas_call | solution.py:428
  29.6 3.2 %shard_map.56 = f32[1,144,1024]{2,1,0:T(8,128)} custom-call(s32[1,12]{1,0:T(1,128)} %counts_ref.1, s32[12,1,48]{2,1,0:T(1,128)} %bitcast.10, s32[12,1,48]{2,1,0:T(1,128)} %bitcast.11, f32[3,192,256]{2,1,0:T(8,128)} %shard_map.55.cc_ref), custom_call_target="tpu_custom_call" | custom-call | tf_op jit(solution)/shard_map/pallas_call | solution.py:452

commit v5 on v4

--- a/solution.py
+++ b/solution.py
@@ -265,47 +265,42 @@
                 part = pool32[h, pl.ds(m, pool, stride=blocks_in), :].astype(jnp.bfloat16)
                 pool16[m, :, h * HALF : (h + 1) * HALF] = part
 
-        def one(j, carry):
-            empty = jnp.zeros((pool, BLOCK), jnp.bfloat16)
-            left = jnp.concatenate(
-                [
-                    jnp.concatenate(
-                        [
-                            pool16[s - q] if 0 <= s - q < blocks_in else empty
-                            for s in range(first_s, last_s + 1)
-                        ],
-                        axis=1,
-                    )
-                    for q in reversed(range(lag_blocks))
-                ],
-                axis=0,
-            )
-            index = own_count * n + j
-            right = jnp.concatenate(
-                [
-                    hankel[index, :, lane : lane + BLOCK]
-                    for s in range(first_s, last_s + 1)
-                    for lane in ((2 * s - first_chunk) * HALF, (2 * s + 1 - first_chunk) * HALF)
-                ],
-                axis=0,
-            )
-            term = jnp.dot(left, right, preferred_element_type=jnp.float32)
-
-            @pl.when(n == 0)
-            def _():
-                cc_ref[j] = term
-
-            @pl.when(n > 0)
-            def _():
-                cc_ref[j] += term
-
-            @pl.when((n == 2) & (j == own_count - 2))
-            def _():
-                forward_diag(3)
-
-            return carry
-
-        lax.fori_loop(0, own_count, one, 0)
+        pl.when(n == 2)(functools.partial(forward_diag, 3))
+        empty = jnp.zeros((pool, BLOCK), jnp.bfloat16)
+        left = jnp.concatenate(
+            [
+                jnp.concatenate(
+                    [
+                        pool16[s - q] if 0 <= s - q < blocks_in else empty
+                        for s in range(first_s, last_s + 1)
+                    ],
+                    axis=1,
+                )
+                for q in reversed(range(lag_blocks))
+            ],
+            axis=0,
+        )
+        right = jnp.concatenate(
+            [
+                jnp.concatenate(
+                    [hankel[own_count * n + j, :, lane : lane + BLOCK] for j in range(own_count)], axis=1
+                )
+                for s in range(first_s, last_s + 1)
+                for lane in ((2 * s - first_chunk) * HALF, (2 * s + 1 - first_chunk) * HALF)
+            ],
+            axis=0,
+        )
+        term = jnp.dot(left, right, preferred_element_type=jnp.float32)
+
+        @pl.when(n == 0)
+        def _():
+            for j in range(own_count):
+                cc_ref[j] = term[:, j * BLOCK : (j + 1) * BLOCK]
+
+        @pl.when(n > 0)
+        def _():
+            for j in range(own_count):
+                cc_ref[j] += term[:, j * BLOCK : (j + 1) * BLOCK]
 
     own_near.start()
 
@@ -392,23 +387,29 @@
 
 
 def select_kernel(scale, own_count, comps, lag_blocks, counts_ref, partners_ref, codes_ref, cc_ref, out_ref):
-    trace = own_count * lax.axis_index("tm") + pl.program_id(0)
     pool = cc_ref.shape[1] // lag_blocks
     slots = partners_ref.shape[2]
     pool_row = lax.broadcasted_iota(jnp.int32, (pool, slots), 0)
     slot_lane = lax.broadcasted_iota(jnp.int32, (pool, slots), 1)
     dims = (((0,), (0,)), ((), ()))
-    wanted = partners_ref[trace] * comps + codes_ref[trace]
-    hit = (wanted == pool_row) & (slot_lane < counts_ref[0, trace])
-    chosen = jnp.where(hit, 1.0, 0.0).astype(jnp.bfloat16)
-    for q in range(lag_blocks):
-        part = cc_ref[0, q * pool : (q + 1) * pool, :]
-        high = part.astype(jnp.bfloat16)
-        low = (part - high.astype(jnp.float32)).astype(jnp.bfloat16)
-        total = lax.dot_general(chosen, low, dims, preferred_element_type=jnp.float32)
-        total += lax.dot_general(chosen, high, dims, preferred_element_type=jnp.float32)
-        lag = (lag_blocks - 1 - q) * BLOCK
-        out_ref[0, :, lag : lag + BLOCK] = total * scale
+
+    def one(j, carry):
+        trace = own_count * lax.axis_index("tm") + j
+        wanted = partners_ref[trace] * comps + codes_ref[trace]
+        hit = (wanted == pool_row) & (slot_lane < counts_ref[0, trace])
+        chosen = jnp.where(hit, 1.0, 0.0).astype(jnp.bfloat16)
+        rows = pl.ds(pl.multiple_of(j * slots, 8), slots)
+        for q in range(lag_blocks):
+            part = cc_ref[j, q * pool : (q + 1) * pool, :]
+            high = part.astype(jnp.bfloat16)
+            low = (part - high.astype(jnp.float32)).astype(jnp.bfloat16)
+            total = lax.dot_general(chosen, low, dims, preferred_element_type=jnp.float32)
+            total += lax.dot_general(chosen, high, dims, preferred_element_type=jnp.float32)
+            lag = (lag_blocks - 1 - q) * BLOCK
+            out_ref[0, rows, lag : lag + BLOCK] = total * scale
+        return carry
+
+    lax.fori_loop(0, own_count, one, 0)
 
 
 def gathered_shards(record, requested, partners, codes, counts):
@@ -454,9 +455,8 @@
             select_kernel, 1.0 / math.sqrt(window_len * windows), own_count, comps, lag_blocks
         ),
         out_shape=jax.ShapeDtypeStruct((1, own_count * slots, LAGS), jnp.float32),
-        grid=(own_count,),
-        in_specs=[smem, vmem, vmem, pl.BlockSpec((1, lag_blocks * pool, BLOCK), lambda j: (j, 0, 0))],
-        out_specs=pl.BlockSpec((1, slots, LAGS), lambda j: (0, j, 0)),
+        in_specs=[smem, vmem, vmem, vmem],
+        out_specs=vmem,
         compiler_params=pltpu.CompilerParams(vmem_limit_bytes=60 * 1024 * 1024),
     )(counts, partners.transpose(1, 0, 2), codes.transpose(1, 0, 2), cc)
 

time: 33 us -> 32.6 us (0.988)
    pallas_call x1, Pallas kernels: 3.15 us -> 2.68 us  [gathered_shards(): pl.pallas_call(functools.partial(select_kernel, 1.0 / math.sqrt(window_le...]
where the time goes in v5:
time: 32.6 us; the launch traced here: 32.4 us
  Pallas kernels  32.4 us (99%)
    pallas_call x1, Pallas kernels, gathered_shards(): pl.pallas_call(functools.partial(exchange_kernel, dims), out_shape=cc_sha...  29.7 us
    pallas_call x1, Pallas kernels, gathered_shards(): pl.pallas_call(functools.partial(select_kernel, 1.0 / math.sqrt(window_le...  2.68 us

profile of v5, /device:TPU:0, one launch (start us, length us, event | category | flops | bytes accessed | tf_op | source)
XLA Modules:
  0.0 32.4 jit_solution(5953862832099890046)
XLA Ops:
  0.0 29.7 %shard_map.55.cc_ref = f32[3,192,256]{2,1,0:T(8,128)} custom-call(s32[8,2,8]{2,1,0:T(2,128)} %bitcast.9, bf16[3,4,4096]{2,1,0:T(4,128)(2,1)} %bitcast.8), custom_call_target="tpu_custom_call" | custom-call | tf_op jit(solution)/shard_map/pallas_call | solution.py:429
  29.7 2.7 %shard_map.56 = f32[1,144,1024]{2,1,0:T(8,128)} custom-call(s32[1,12]{1,0:T(1,128)} %counts_ref.1, s32[12,1,48]{2,1,0:T(1,128)} %bitcast.10, s32[12,1,48]{2,1,0:T(1,128)} %bitcast.11, f32[3,192,256]{2,1,0:T(8,128)} %shard_map.55.cc_ref), custom_call_target="tpu_custom_call" | custom-call | tf_op jit(solution)/shard_map/pallas_call | solution.py:453

commit v6 on v5

--- a/solution.py
+++ b/solution.py
@@ -80,7 +80,7 @@
 MESH = pl.DeviceIdType.MESH
 HALF = 128
 BLOCK = 2 * HALF
-FROM_X, FROM_Y, DIAG_A, DIAG_B, CORE_OWN, CORE_X, CORE_Y, CORE_D = range(8)
+X_A, X_B, Y_A, Y_B, DIAG_A, DIAG_B, CORE_OWN, CORE_X, CORE_Y, CORE_D = range(10)
 
 
 def exchange_kernel(
@@ -143,9 +143,9 @@
 
     def plane_copy(k, kind, origin, target):
         blk = blks[k]
-        if kind == DIAG_A:
+        if kind in (X_A, Y_A, DIAG_A):
             ref = blk.at[origin, pl.ds(0, traces // 2)]
-        elif kind == DIAG_B:
+        elif kind in (X_B, Y_B, DIAG_B):
             ref = blk.at[origin, pl.ds(traces // 2, traces // 2)]
         else:
             ref = blk.at[origin]
@@ -155,34 +155,44 @@
             device_id=(t, target), device_id_type=MESH,
         )
 
-    def z_copy(index, source, slot, target):
-        return pltpu.make_async_remote_copy(
-            src_ref=blks[source].at[e], dst_ref=blks[slot].at[e],
-            send_sem=zsend.at[index], recv_sem=zrecv.at[slot - 1],
-            device_id=(target, e), device_id_type=MESH,
-        )
-
-    own_near = z_copy(0, 0, 1, near)
-    own_far = z_copy(1, 0, 2, far)
-    near_to_far = z_copy(2, 1, 3, far)
-    far_to_near = z_copy(3, 2, 2, near)
-    rest_to_near = z_copy(4, 3, 3, near)
-
-    def wait_window(k):
-        z_copy(0, 0, k, near).wait_recv()
-
-    def send_own(k):
-        plane_copy(k, FROM_X, e, ex).start()
-        plane_copy(k, FROM_Y, e, ey).start()
+    def z_copies(index, source, slot, target):
+        halves = []
+        for half in (0, 1):
+            part = pl.ds(half * (traces // 2), traces // 2)
+            halves.append(
+                pltpu.make_async_remote_copy(
+                    src_ref=blks[source].at[e, part], dst_ref=blks[slot].at[e, part],
+                    send_sem=zsend.at[index, half], recv_sem=zrecv.at[slot - 1, half],
+                    device_id=(target, e), device_id_type=MESH,
+                )
+            )
+        return halves
+
+    own_near = z_copies(0, 0, 1, near)
+    own_far = z_copies(1, 0, 2, far)
+    near_to_far = z_copies(2, 1, 3, far)
+    far_to_near = z_copies(3, 2, 2, near)
+    rest_to_near = z_copies(4, 3, 3, near)
+
+    def wait_half(k, half):
+        z_copies(0, 0, k, near)[half].wait_recv()
+
+    def send_half(k, half):
+        plane_copy(k, (X_A, X_B)[half], e, ex).start()
+        plane_copy(k, (Y_A, Y_B)[half], e, ey).start()
+
+    def send_core(k):
         plane_copy(k, CORE_OWN, e, ec).start()
 
     def forward_xy(k):
-        plane_copy(k, FROM_X, ex, ex).wait_recv()
+        plane_copy(k, X_A, ex, ex).wait_recv()
         plane_copy(k, DIAG_A, ex, ey).start()
-        plane_copy(k, CORE_X, ex, ec).start()
-        plane_copy(k, FROM_Y, ey, ey).wait_recv()
+        plane_copy(k, Y_A, ey, ey).wait_recv()
+        plane_copy(k, Y_B, ey, ey).wait_recv()
         plane_copy(k, DIAG_B, ey, ex).start()
         plane_copy(k, CORE_Y, ey, ec).start()
+        plane_copy(k, X_B, ex, ex).wait_recv()
+        plane_copy(k, CORE_X, ex, ec).start()
 
     def forward_diag(k):
         plane_copy(k, DIAG_A, ed, ey).wait_recv()
@@ -265,7 +275,8 @@
                 part = pool32[h, pl.ds(m, pool, stride=blocks_in), :].astype(jnp.bfloat16)
                 pool16[m, :, h * HALF : (h + 1) * HALF] = part
 
-        pl.when(n == 2)(functools.partial(forward_diag, 3))
+        pl.when(n == 0)(functools.partial(forward_diag, 1))
+        pl.when(n == 1)(functools.partial(forward_xy, 3))
         empty = jnp.zeros((pool, BLOCK), jnp.bfloat16)
         left = jnp.concatenate(
             [
@@ -302,56 +313,66 @@
             for j in range(own_count):
                 cc_ref[j] += term[:, j * BLOCK : (j + 1) * BLOCK]
 
-    own_near.start()
-
-    @pl.when(inner)
-    def _():
-        own_far.start()
-
-    send_own(0)
+    for half in (0, 1):
+        own_near[half].start()
+        send_half(0, half)
+
+        @pl.when(inner)
+        def _():
+            own_far[half].start()
+
+    send_core(0)
+
     def before_build(n):
         if n == 1:
-            wait_window(1)
-
-            @pl.when(inner)
-            def _():
-                near_to_far.start()
-                wait_window(2)
-                far_to_near.start()
-
-            send_own(1)
+            for half in (0, 1):
+                wait_half(1, half)
+                send_half(1, half)
+
+                @pl.when(inner)
+                def _():
+                    near_to_far[half].start()
+                    wait_half(2, half)
+                    far_to_near[half].start()
+
+            send_core(1)
             forward_xy(0)
         if n == 2:
+            for half in (0, 1):
+
+                @pl.when(jnp.logical_not(inner))
+                def _():
+                    wait_half(2, half)
+
+                @pl.when(inner)
+                def _():
+                    wait_half(3, half)
+                    rest_to_near[half].start()
+
+                send_half(2, half)
+            send_core(2)
             forward_diag(0)
-
-            @pl.when(jnp.logical_not(inner))
-            def _():
-                wait_window(2)
-
-            @pl.when(inner)
-            def _():
-                wait_window(3)
-                rest_to_near.start()
-
-            send_own(2)
             forward_xy(1)
-            load_asked.wait()
         if n == 3:
-            forward_diag(1)
-
-            @pl.when(jnp.logical_not(inner))
-            def _():
-                wait_window(3)
-
-            send_own(3)
             forward_xy(2)
         if n == 4:
-            forward_diag(2)
-            forward_xy(3)
+            forward_diag(3)
         if n < 4:
             unmirror(n)
 
     def before_correlate(n):
+        if n == 0:
+            for half in (0, 1):
+
+                @pl.when(jnp.logical_not(inner))
+                def _():
+                    wait_half(3, half)
+
+                send_half(3, half)
+            send_core(3)
+            load_asked.wait()
+        if n == 1:
+            forward_diag(2)
         wait_core(n)
         pick(n)
 
@@ -366,18 +387,21 @@
 
     lax.fori_loop(0, 6, step, 0)
 
-    own_near.wait_send()
-
-    @pl.when(inner)
-    def _():
-        own_far.wait_send()
-        near_to_far.wait_send()
-        far_to_near.wait_send()
-        rest_to_near.wait_send()
+    for half in (0, 1):
+        own_near[half].wait_send()
+
+        @pl.when(inner)
+        def _():
+            own_far[half].wait_send()
+            near_to_far[half].wait_send()
+            far_to_near[half].wait_send()
+            rest_to_near[half].wait_send()
 
     for k in range(4):
-        plane_copy(k, FROM_X, e, ex).wait_send()
-        plane_copy(k, FROM_Y, e, ey).wait_send()
+        plane_copy(k, X_A, e, ex).wait_send()
+        plane_copy(k, X_B, e, ex).wait_send()
+        plane_copy(k, Y_A, e, ey).wait_send()
+        plane_copy(k, Y_B, e, ey).wait_send()
         plane_copy(k, CORE_OWN, e, ec).wait_send()
         plane_copy(k, DIAG_A, ex, ey).wait_send()
         plane_copy(k, CORE_X, ex, ec).wait_send()
@@ -440,10 +464,10 @@
             pltpu.VMEM((own_count, blocks_in, BLOCK), jnp.float32),
             pltpu.VMEM((blocks_in, pool, BLOCK), jnp.bfloat16),
             pltpu.VMEM((4 * own_count, HALF, depth + HALF), jnp.bfloat16),
-            pltpu.SemaphoreType.DMA((4, 8)),
-            pltpu.SemaphoreType.DMA((4, 8)),
-            pltpu.SemaphoreType.DMA((5,)),
-            pltpu.SemaphoreType.DMA((3,)),
+            pltpu.SemaphoreType.DMA((4, 10)),
+            pltpu.SemaphoreType.DMA((4, 10)),
+            pltpu.SemaphoreType.DMA((5, 2)),
+            pltpu.SemaphoreType.DMA((3, 2)),
             pltpu.SemaphoreType.DMA((2,)),
         ],
         compiler_params=pltpu.CompilerParams(

time: 32.6 us -> 34.4 us (1.055)
  Pallas kernels: 32.4 us -> 34.2 us
    pallas_call x1, Pallas kernels: 29.7 us -> 31.5 us  [gathered_shards(): pl.pallas_call(functools.partial(exchange_kernel, dims), out_shape=cc_sha...]
where the time goes in v6:
time: 34.4 us; the launch traced here: 34.2 us
  Pallas kernels  34.2 us (99%)
    pallas_call x1, Pallas kernels, gathered_shards(): pl.pallas_call(functools.partial(exchange_kernel, dims), out_shape=cc_sha...  31.5 us
    pallas_call x1, Pallas kernels, gathered_shards(): pl.pallas_call(functools.partial(select_kernel, 1.0 / math.sqrt(window_le...  2.68 us

profile of v6, /device:TPU:0, one launch (start us, length us, event | category | flops | bytes accessed | tf_op | source)
XLA Modules:
  0.0 34.2 jit_solution(16884014442304605651)
XLA Ops:
  0.0 31.5 %shard_map.55.cc_ref = f32[3,192,256]{2,1,0:T(8,128)} custom-call(s32[8,2,8]{2,1,0:T(2,128)} %bitcast.9, bf16[3,4,4096]{2,1,0:T(4,128)(2,1)} %bitcast.8), custom_call_target="tpu_custom_call" | custom-call | tf_op jit(solution)/shard_map/pallas_call | solution.py:453
  31.5 2.7 %shard_map.56 = f32[1,144,1024]{2,1,0:T(8,128)} custom-call(s32[1,12]{1,0:T(1,128)} %counts_ref.1, s32[12,1,48]{2,1,0:T(1,128)} %bitcast.10, s32[12,1,48]{2,1,0:T(1,128)} %bitcast.11, f32[3,192,256]{2,1,0:T(8,128)} %shard_map.55.cc_ref), custom_call_target="tpu_custom_call" | custom-call | tf_op jit(solution)/shard_map/pallas_call | solution.py:477

commit v7 on v5

--- a/solution.py
+++ b/solution.py
@@ -202,10 +202,11 @@
     last_chunk = 2 * last_s + 2
 
     def unmirror(k):
-        for j in range(own_count):
-            for h in (0, 1):
-                lanes = slice(h * HALF, (h + 1) * HALF)
-                own32[j, :, lanes] = flip_halves(blks[k][e, own_count * t + j, :, lanes])
+        for h in (0, 1):
+            lanes = slice(h * HALF, (h + 1) * HALF)
+            own = blks[k][e, pl.ds(own_count * t, own_count), :, lanes]
+            flipped = flip_halves(own.reshape(own_count * blocks_in, HALF))
+            own32[:, :, lanes] = flipped.reshape(own_count, blocks_in, HALF)
 
     def build(n):
         def one(j, carry):
@@ -257,7 +258,7 @@
                 pool32[h, pl.ds(start, comps * blocks_in), :] = rows[:, h * HALF : (h + 1) * HALF]
             return carry
 
-        lax.fori_loop(0, owners * capacity, one, 0)
+        lax.fori_loop(0, owners * capacity, one, 0, unroll=4)
 
     def correlate(n):
         for m in range(blocks_in):
@@ -386,19 +387,25 @@
         plane_copy(k, CORE_D, ed, ec).wait_send()
 
 
-def select_kernel(scale, own_count, comps, lag_blocks, counts_ref, partners_ref, codes_ref, cc_ref, out_ref):
+def select_kernel(scale, own_count, comps, lag_blocks, counts_ref, partners_ref, codes_ref, cc_hbm, out_hbm, cc_ref, out_ref, fetched, written):
+    fetches = [
+        pltpu.make_async_copy(cc_hbm.at[j], cc_ref.at[j], fetched.at[j]) for j in range(own_count)
+    ]
+    for fetch in fetches:
+        fetch.start()
+    writes = []
     pool = cc_ref.shape[1] // lag_blocks
     slots = partners_ref.shape[2]
     pool_row = lax.broadcasted_iota(jnp.int32, (pool, slots), 0)
     slot_lane = lax.broadcasted_iota(jnp.int32, (pool, slots), 1)
     dims = (((0,), (0,)), ((), ()))
 
-    def one(j, carry):
+    for j in range(own_count):
         trace = own_count * lax.axis_index("tm") + j
         wanted = partners_ref[trace] * comps + codes_ref[trace]
         hit = (wanted == pool_row) & (slot_lane < counts_ref[0, trace])
         chosen = jnp.where(hit, 1.0, 0.0).astype(jnp.bfloat16)
-        rows = pl.ds(pl.multiple_of(j * slots, 8), slots)
+        fetches[j].wait()
         for q in range(lag_blocks):
             part = cc_ref[j, q * pool : (q + 1) * pool, :]
             high = part.astype(jnp.bfloat16)
@@ -406,10 +413,15 @@
             total = lax.dot_general(chosen, low, dims, preferred_element_type=jnp.float32)
             total += lax.dot_general(chosen, high, dims, preferred_element_type=jnp.float32)
             lag = (lag_blocks - 1 - q) * BLOCK
-            out_ref[0, rows, lag : lag + BLOCK] = total * scale
-        return carry
-
-    lax.fori_loop(0, own_count, one, 0)
+            out_ref[j, :, lag : lag + BLOCK] = total * scale
+        writes.append(
+            pltpu.make_async_copy(
+                out_ref.at[j], out_hbm.at[0, pl.ds(j * slots, slots)], written.at[j]
+            )
+        )
+        writes[j].start()
+    for write in writes:
+        write.wait()
 
 
 def gathered_shards(record, requested, partners, codes, counts):
@@ -455,8 +467,14 @@
             select_kernel, 1.0 / math.sqrt(window_len * windows), own_count, comps, lag_blocks
         ),
         out_shape=jax.ShapeDtypeStruct((1, own_count * slots, LAGS), jnp.float32),
-        in_specs=[smem, vmem, vmem, vmem],
-        out_specs=vmem,
+        in_specs=[smem, vmem, vmem, pl.BlockSpec(memory_space=pltpu.HBM)],
+        out_specs=pl.BlockSpec(memory_space=pltpu.HBM),
+        scratch_shapes=[
+            pltpu.VMEM(cc_shape.shape, jnp.float32),
+            pltpu.VMEM((own_count, slots, LAGS), jnp.float32),
+            pltpu.SemaphoreType.DMA((own_count,)),
+            pltpu.SemaphoreType.DMA((own_count,)),
+        ],
         compiler_params=pltpu.CompilerParams(vmem_limit_bytes=60 * 1024 * 1024),
     )(counts, partners.transpose(1, 0, 2), codes.transpose(1, 0, 2), cc)
 

time: 32.6 us -> 32.7 us (level)
    pallas_call x1, Pallas kernels: 2.68 us -> 3.08 us  [gathered_shards(): pl.pallas_call(functools.partial(select_kernel, 1.0 / math.sqrt(window_le...]
where the time goes in v7:
time: 32.7 us; the launch traced here: 32.5 us
  Pallas kernels  32.5 us (99%)
    pallas_call x1, Pallas kernels, gathered_shards(): pl.pallas_call(functools.partial(exchange_kernel, dims), out_shape=cc_sha...  29.4 us
    pallas_call x1, Pallas kernels, gathered_shards(): pl.pallas_call(functools.partial(select_kernel, 1.0 / math.sqrt(window_le...  3.08 us

profile of v7, /device:TPU:0, one launch (start us, length us, event | category | flops | bytes accessed | tf_op | source)
XLA Modules:
  0.0 32.5 jit_solution(2363682627869269080)
XLA Ops:
  0.0 29.4 %shard_map.55.cc_hbm = f32[3,192,256]{2,1,0:T(8,128)} custom-call(s32[8,2,8]{2,1,0:T(2,128)} %bitcast.9, bf16[3,4,4096]{2,1,0:T(4,128)(2,1)} %bitcast.8), custom_call_target="tpu_custom_call" | custom-call | tf_op jit(solution)/shard_map/pallas_call | solution.py:441
  29.4 3.1 %shard_map.56 = f32[1,144,1024]{2,1,0:T(8,128)} custom-call(s32[1,12]{1,0:T(1,128)} %counts_ref.1, s32[12,1,48]{2,1,0:T(1,128)} %bitcast.10, s32[12,1,48]{2,1,0:T(1,128)} %bitcast.11, f32[3,192,256]{2,1,0:T(8,128)} %shard_map.55.cc_hbm), custom_call_target="tpu_custom_call" | custom-call | tf_op jit(solution)/shard_map/pallas_call | solution.py:465

commit v8 on v5

--- a/solution.py
+++ b/solution.py
@@ -84,12 +84,13 @@
 
 
 def exchange_kernel(
-    dims, asked_hbm, record_hbm, cc_ref, *scratch
+    dims, scale, asked_hbm, record_hbm, counts_hbm, partners_hbm, codes_hbm, out_ref, *scratch
 ):
     traces, blocks_in, owners, capacity, comps, own_count, lag_blocks = dims
     blks = scratch[:4]
     (asked_ref, record_ref, rows32, pool32, own32, pool16, hankel) = scratch[4:11]
-    (send, recv, zsend, zrecv, local) = scratch[11:]
+    (send, recv, zsend, zrecv, local) = scratch[11:16]
+    (cc_ref, counts_ref, partners_ref, codes_ref) = scratch[16:]
     pool = owners * capacity * comps
     first_s, last_s = 1, blocks_in + lag_blocks - 3
     t = lax.axis_index("tm")
@@ -104,8 +105,15 @@
 
     load_asked = pltpu.make_async_copy(asked_hbm, asked_ref, local.at[0])
     load_record = pltpu.make_async_copy(record_hbm, record_ref, local.at[1])
+    tables = [
+        pltpu.make_async_copy(counts_hbm, counts_ref, local.at[2]),
+        pltpu.make_async_copy(partners_hbm, partners_ref, local.at[3]),
+        pltpu.make_async_copy(codes_hbm, codes_ref, local.at[4]),
+    ]
     load_record.start()
     load_asked.start()
+    for table in tables:
+        table.start()
     barrier = pltpu.get_barrier_semaphore()
     for peer in ((t, ex), (t, ey), (t, ec), (near, e), (far, e)):
         pl.semaphore_signal(barrier, inc=1, device_id=peer, device_id_type=MESH)
@@ -366,35 +374,15 @@
 
     lax.fori_loop(0, 6, step, 0)
 
-    own_near.wait_send()
-
-    @pl.when(inner)
-    def _():
-        own_far.wait_send()
-        near_to_far.wait_send()
-        far_to_near.wait_send()
-        rest_to_near.wait_send()
-
-    for k in range(4):
-        plane_copy(k, FROM_X, e, ex).wait_send()
-        plane_copy(k, FROM_Y, e, ey).wait_send()
-        plane_copy(k, CORE_OWN, e, ec).wait_send()
-        plane_copy(k, DIAG_A, ex, ey).wait_send()
-        plane_copy(k, CORE_X, ex, ec).wait_send()
-        plane_copy(k, DIAG_B, ey, ex).wait_send()
-        plane_copy(k, CORE_Y, ey, ec).wait_send()
-        plane_copy(k, CORE_D, ed, ec).wait_send()
-
-
-def select_kernel(scale, own_count, comps, lag_blocks, counts_ref, partners_ref, codes_ref, cc_ref, out_ref):
-    pool = cc_ref.shape[1] // lag_blocks
+    for table in tables:
+        table.wait()
     slots = partners_ref.shape[2]
     pool_row = lax.broadcasted_iota(jnp.int32, (pool, slots), 0)
     slot_lane = lax.broadcasted_iota(jnp.int32, (pool, slots), 1)
     dims = (((0,), (0,)), ((), ()))
 
-    def one(j, carry):
-        trace = own_count * lax.axis_index("tm") + j
+    def select(j, carry):
+        trace = own_count * t + j
         wanted = partners_ref[trace] * comps + codes_ref[trace]
         hit = (wanted == pool_row) & (slot_lane < counts_ref[0, trace])
         chosen = jnp.where(hit, 1.0, 0.0).astype(jnp.bfloat16)
@@ -409,7 +397,26 @@
             out_ref[0, rows, lag : lag + BLOCK] = total * scale
         return carry
 
-    lax.fori_loop(0, own_count, one, 0)
+    lax.fori_loop(0, own_count, select, 0)
+
+    own_near.wait_send()
+
+    @pl.when(inner)
+    def _():
+        own_far.wait_send()
+        near_to_far.wait_send()
+        far_to_near.wait_send()
+        rest_to_near.wait_send()
+
+    for k in range(4):
+        plane_copy(k, FROM_X, e, ex).wait_send()
+        plane_copy(k, FROM_Y, e, ey).wait_send()
+        plane_copy(k, CORE_OWN, e, ec).wait_send()
+        plane_copy(k, DIAG_A, ex, ey).wait_send()
+        plane_copy(k, CORE_X, ex, ec).wait_send()
+        plane_copy(k, DIAG_B, ey, ex).wait_send()
+        plane_copy(k, CORE_Y, ey, ec).wait_send()
+        plane_copy(k, CORE_D, ed, ec).wait_send()
 
 
 def gathered_shards(record, requested, partners, codes, counts):
@@ -425,11 +432,10 @@
     cc_shape = jax.ShapeDtypeStruct((own_count, lag_blocks * pool, BLOCK), jnp.float32)
     dims = (traces, blocks_in, owners, capacity, comps, own_count, lag_blocks)
     vmem = pl.BlockSpec(memory_space=pltpu.VMEM)
-    smem = pl.BlockSpec(memory_space=pltpu.SMEM)
-    cc = pl.pallas_call(
-        functools.partial(exchange_kernel, dims),
-        out_shape=cc_shape,
-        in_specs=[pl.BlockSpec(memory_space=pltpu.HBM)] * 2,
+    return pl.pallas_call(
+        functools.partial(exchange_kernel, dims, 1.0 / math.sqrt(window_len * windows)),
+        out_shape=jax.ShapeDtypeStruct((1, own_count * slots, LAGS), jnp.float32),
+        in_specs=[pl.BlockSpec(memory_space=pltpu.HBM)] * 5,
         out_specs=vmem,
         scratch_shapes=[pltpu.VMEM((owners, traces, blocks_in, BLOCK), jnp.bfloat16)] * 4
         + [
@@ -444,21 +450,22 @@
             pltpu.SemaphoreType.DMA((4, 8)),
             pltpu.SemaphoreType.DMA((5,)),
             pltpu.SemaphoreType.DMA((3,)),
-            pltpu.SemaphoreType.DMA((2,)),
+            pltpu.SemaphoreType.DMA((5,)),
+            pltpu.VMEM(cc_shape.shape, jnp.float32),
+            pltpu.SMEM(counts.shape, jnp.int32),
+            pltpu.VMEM((traces, 1, slots), jnp.int32),
+            pltpu.VMEM((traces, 1, slots), jnp.int32),
         ],
         compiler_params=pltpu.CompilerParams(
             collective_id=0, has_side_effects=True, vmem_limit_bytes=60 * 1024 * 1024
         ),
-    )(requested.transpose(0, 2, 1), record.transpose(2, 1, 0, 3)[0])
-    return pl.pallas_call(
-        functools.partial(
-            select_kernel, 1.0 / math.sqrt(window_len * windows), own_count, comps, lag_blocks
-        ),
-        out_shape=jax.ShapeDtypeStruct((1, own_count * slots, LAGS), jnp.float32),
-        in_specs=[smem, vmem, vmem, vmem],
-        out_specs=vmem,
-        compiler_params=pltpu.CompilerParams(vmem_limit_bytes=60 * 1024 * 1024),
-    )(counts, partners.transpose(1, 0, 2), codes.transpose(1, 0, 2), cc)
+    )(
+        requested.transpose(0, 2, 1),
+        record.transpose(2, 1, 0, 3)[0],
+        counts,
+        partners.transpose(1, 0, 2),
+        codes.transpose(1, 0, 2),
+    )
 
 
 def solution(mesh):

time: 32.6 us -> 32.6 us (level)
  local copies, waits for them, and re-layouts: 0 us -> 1.93 us
  Pallas kernels: 32.4 us -> 30.5 us
    unnamed x0 -> x1, local copies, waits for them, and re-layouts: none -> 1.93 us
    pallas_call x2 -> x1, Pallas kernels: 32.4 us -> 30.5 us  [gathered_shards(): pl.pallas_call(functools.partial(exchange_kernel, dims, 1.0 / math.sqrt(w...]
where the time goes in v8:
time: 32.6 us; the launch traced here: 32.4 us
  Pallas kernels  30.5 us (94%)
  local copies, waits for them, and re-layouts  1.93 us (6%)
    pallas_call x1, Pallas kernels, gathered_shards(): pl.pallas_call(functools.partial(exchange_kernel, dims, 1.0 / math.sqrt(w...  30.5 us
    unnamed x1, local copies, waits for them, and re-layouts  1.93 us

profile of v8, /device:TPU:0, one launch (start us, length us, event | category | flops | bytes accessed | tf_op | source)
XLA Modules:
  0.0 32.4 jit_solution(17950743563548994091)
XLA Ops:
  0.0 30.5 %shard_map.55 = f32[1,144,1024]{2,1,0:T(8,128)} custom-call(s32[8,2,8]{2,1,0:T(2,128)} %bitcast.9, bf16[3,4,4096]{2,1,0:T(4,128)(2,1)} %bitcast.8, s32[1,12]{1,0:T(1,128)} %counts_hbm.1, s32[12,1,48]{2,1,0:T(1,128)} %bitcast.10, s32[12,1,48]{2,1,0:T(1,128)} %bitcast.11), custom_call_target="tpu_custom_call" | custom-call | tf_op jit(solution)/shard_map/pallas_call | solution.py:435
  30.5 1.9 %copy.8 = f32[1,144,1024]{2,1,0:T(8,128)} copy(f32[1,144,1024]{2,1,0:T(8,128)} %shard_map.55) | data formatting | bytes 1179648

commit v9 on v5

--- a/solution.py
+++ b/solution.py
@@ -84,12 +84,12 @@
 
 
 def exchange_kernel(
-    dims, asked_hbm, record_hbm, cc_ref, *scratch
+    dims, asked_ref, record_ref, cc_ref, *scratch
 ):
     traces, blocks_in, owners, capacity, comps, own_count, lag_blocks = dims
     blks = scratch[:4]
-    (asked_ref, record_ref, rows32, pool32, own32, pool16, hankel) = scratch[4:11]
-    (send, recv, zsend, zrecv, local) = scratch[11:]
+    (rows32, pool32, own32, pool16, hankel) = scratch[4:9]
+    (send, recv, zsend, zrecv) = scratch[9:]
     pool = owners * capacity * comps
     first_s, last_s = 1, blocks_in + lag_blocks - 3
     t = lax.axis_index("tm")
@@ -102,10 +102,6 @@
     near, far = t + 1 - 2 * lax.rem(t, 2), 3 - t
     inner = (t == 1) | (t == 2)
 
-    load_asked = pltpu.make_async_copy(asked_hbm, asked_ref, local.at[0])
-    load_record = pltpu.make_async_copy(record_hbm, record_ref, local.at[1])
-    load_record.start()
-    load_asked.start()
     barrier = pltpu.get_barrier_semaphore()
     for peer in ((t, ex), (t, ey), (t, ec), (near, e), (far, e)):
         pl.semaphore_signal(barrier, inc=1, device_id=peer, device_id_type=MESH)
@@ -118,7 +114,6 @@
         return jnp.dot(tile, mirror, preferred_element_type=jnp.float32)
 
     stations = traces // comps
-    load_record.wait()
 
     def whiten(comp, carry):
         values = record_ref[comp].astype(jnp.float32)
@@ -335,7 +330,6 @@
 
             send_own(2)
             forward_xy(1)
-            load_asked.wait()
         if n == 3:
             forward_diag(1)
 
@@ -429,12 +423,10 @@
     cc = pl.pallas_call(
         functools.partial(exchange_kernel, dims),
         out_shape=cc_shape,
-        in_specs=[pl.BlockSpec(memory_space=pltpu.HBM)] * 2,
+        in_specs=[smem, vmem],
         out_specs=vmem,
         scratch_shapes=[pltpu.VMEM((owners, traces, blocks_in, BLOCK), jnp.bfloat16)] * 4
         + [
-            pltpu.SMEM((owners, capacity, owners), jnp.int32),
-            pltpu.VMEM((comps, stations, window_len), jnp.bfloat16),
             pltpu.VMEM((2, traces * blocks_in, HALF), jnp.float32),
             pltpu.VMEM((2, pool * blocks_in, HALF), jnp.float32),
             pltpu.VMEM((own_count, blocks_in, BLOCK), jnp.float32),
@@ -444,10 +436,9 @@
             pltpu.SemaphoreType.DMA((4, 8)),
             pltpu.SemaphoreType.DMA((5,)),
             pltpu.SemaphoreType.DMA((3,)),
-            pltpu.SemaphoreType.DMA((2,)),
         ],
         compiler_params=pltpu.CompilerParams(
-            collective_id=0, has_side_effects=True, vmem_limit_bytes=60 * 1024 * 1024
+            collective_id=0, has_side_effects=True, vmem_limit_bytes=40 * 1024 * 1024
         ),
     )(requested.transpose(0, 2, 1), record.transpose(2, 1, 0, 3)[0])
     return pl.pallas_call(
@@ -457,7 +448,7 @@
         out_shape=jax.ShapeDtypeStruct((1, own_count * slots, LAGS), jnp.float32),
         in_specs=[smem, vmem, vmem, vmem],
         out_specs=vmem,
-        compiler_params=pltpu.CompilerParams(vmem_limit_bytes=60 * 1024 * 1024),
+        compiler_params=pltpu.CompilerParams(vmem_limit_bytes=16 * 1024 * 1024),
     )(counts, partners.transpose(1, 0, 2), codes.transpose(1, 0, 2), cc)
 
 

time: 32.6 us -> 33.7 us (1.034)
  local copies, waits for them, and re-layouts: 0 us -> 1.6 us
  Pallas kernels: 32.4 us -> 31.9 us
    unnamed x0 -> x10, local copies, waits for them, and re-layouts: none -> 1.6 us
    pallas_call x1, Pallas kernels: 2.68 us -> 2.12 us  [gathered_shards(): pl.pallas_call(functools.partial(select_kernel, 1.0 / math.sqrt(window_le...]
where the time goes in v9:
time: 33.7 us; the launch traced here: 33.5 us
  Pallas kernels  31.9 us (95%)
  local copies, waits for them, and re-layouts  1.6 us (5%)
    pallas_call x1, Pallas kernels, gathered_shards(): pl.pallas_call(functools.partial(exchange_kernel, dims), out_shape=cc_sha...  29.8 us
    pallas_call x1, Pallas kernels, gathered_shards(): pl.pallas_call(functools.partial(select_kernel, 1.0 / math.sqrt(window_le...  2.12 us
    unnamed x10, local copies, waits for them, and re-layouts  1.6 us

profile of v9, /device:TPU:0, one launch (start us, length us, event | category | flops | bytes accessed | tf_op | source)
XLA Modules:
  0.0 33.5 jit_solution(2032349765180059601)
XLA Ops:
  0.0 0.0 copy-start
  0.0 0.9 %copy-done = bf16[4,3,1,4096]{3,0,2,1:T(4,128)(2,1)S(1)} copy-done((bf16[4,3,1,4096]{3,0,2,1:T(4,128)(2,1)S(1)}, bf16[4,3,1,4096]{3,0,2,1:T(4,128)(2,1)}, u32[]{:S(2)}) %copy-start) | copy-done | bytes 98328
  0.9 0.0 copy-start.1
  0.9 0.7 %copy-done.1 = s32[8,8,2]{1,2,0:T(2,128)S(1)} copy-done((s32[8,8,2]{1,2,0:T(2,128)S(1)}, s32[8,8,2]{1,2,0:T(2,128)}, u32[]{:S(2)}) %copy-start.1) | copy-done | bytes 536
  1.6 0.0 copy-start.2
  1.6 0.0 copy-start.3
  1.6 0.0 copy-start.4
  1.6 29.8 %shard_map.55.cc_ref = f32[3,192,256]{2,1,0:T(8,128)S(1)} custom-call(s32[8,2,8]{2,1,0:T(2,128)S(1)} %bitcast.9, bf16[3,4,4096]{2,1,0:T(4,128)(2,1)S(1)} %bitcast.8), custom_call_target="tpu_custom_call" | custom-call | tf_op jit(solution)/shard_map/pallas_call | solution.py:423
  31.4 0.0 copy-done.2
  31.4 0.0 copy-done.3
  31.4 0.0 copy-done.4
  31.4 2.1 %shard_map.56 = f32[1,144,1024]{2,1,0:T(8,128)} custom-call(s32[1,12]{1,0:T(1,128)S(1)} %copy-done.4, s32[12,1,48]{2,1,0:T(1,128)S(1)} %bitcast.10, s32[12,1,48]{2,1,0:T(1,128)S(1)} %bitcast.11, f32[3,192,256]{2,1,0:T(8,128)S(1)} %shard_map.55.cc_ref), custom_call_target="tpu_custom_call" | custom-call | tf_op jit(solution)/shard_map/pallas_call | solution.py:444
Async XLA Ops:
  0.0 0.9 %copy-start = (bf16[4,3,1,4096]{3,0,2,1:T(4,128)(2,1)S(1)}, bf16[4,3,1,4096]{3,0,2,1:T(4,128)(2,1)}, u32[]{:S(2)}) copy-start(bf16[4,3,1,4096]{3,0,2,1:T(4,128)(2,1)} %param.5) | copy-start | bytes 294916
  0.9 0.7 %copy-start.1 = (s32[8,8,2]{1,2,0:T(2,128)S(1)}, s32[8,8,2]{1,2,0:T(2,128)}, u32[]{:S(2)}) copy-start(s32[8,8,2]{1,2,0:T(2,128)} %param.6) | copy-start | bytes 1540
  1.6 29.8 %copy-start.2 = (s32[1,12,48]{2,0,1:T(1,128)S(1)}, s32[1,12,48]{2,0,1:T(1,128)}, u32[]{:S(2)}) copy-start(s32[1,12,48]{2,0,1:T(1,128)} %param.7) | copy-start | bytes 6916
  1.6 29.8 %copy-start.3 = (s32[1,12,48]{2,0,1:T(1,128)S(1)}, s32[1,12,48]{2,0,1:T(1,128)}, u32[]{:S(2)}) copy-start(s32[1,12,48]{2,0,1:T(1,128)} %param.8) | copy-start | bytes 6916
  1.6 29.8 %copy-start.4 = (s32[1,12]{1,0:T(1,128)S(1)}, s32[1,12]{1,0:T(1,128)}, u32[]{:S(2)}) copy-start(s32[1,12]{1,0:T(1,128)} %counts_ref.1) | copy-start | bytes 148
